TPU v7x, 256 devices: a whole 4x4x8 slice. The times are simulated.
256 devices in a mesh: ctx: 64 (over z, y, core), head: 4 (over x).
Axes of the slice: x: 4, y: 4, z: 8, core: 2. Of those that a mesh axis runs over, the one named last changes fastest.
Arguments:
- tokens: bfloat16 [8192, 4096], P('ctx', 'head'), may hold values from -28 to 28
- context_row: int32 [8192], replicated, may hold values from 0 to 8191, as said below
- lengths: int32 [64], replicated, may hold values from 1 to 384, 8192 in all
- q_weight: bfloat16 [4096, 4096], P('ctx', 'head'), may hold values from -0.09375 to 0.09375
- k_weight: bfloat16 [4096, 512], P('ctx', 'head'), may hold values from -0.09375 to 0.09375
- v_weight: bfloat16 [4096, 512], P('ctx', 'head'), may hold values from -0.09375 to 0.09375
- o_weight: bfloat16 [4096, 4096], P('head', 'ctx'), may hold values from -0.09375 to 0.09375
Outputs:
- layer_out: bfloat16 [8192, 4096], P('ctx', 'head')
Inputs may be any that keep to these rules, and one draw needn't show every extreme that they name: `context_row`: a permutation; of the 128 loader rows of one device, at most 3 are rows of one device's 128 packed rows (rows r with the same r // 128), a number reached by some pairs of devices.
All inputs are finite; a program needn't handle non-finite values.
Results may differ from a plain program's by a relative error of at most 0.013.
The roundings to bfloat16 on the way count: a program that leaves them out, or rounds other values in their place, can miss the bound.
Values may be sent and summed in bfloat16 or wider, within the bound.
A program may use at most 64 MiB of HBM per device.

v0:
```python
import math

import jax
import jax.numpy as jnp
from jax import lax
from jax.sharding import PartitionSpec as P

HEADS = 32
KV_HEADS = 4
HD = 128
REACH = 3


ROPE_BASE = 500000.0


def shifted(x, axis, by):
    count = lax.axis_size(axis)
    pairs = [(i, i + by) for i in range(count) if 0 <= i + by < count]
    return lax.ppermute(x, axis, pairs)


def rotate(tensor, positions):
    half_dim = tensor.shape[-1] // 2
    frequency = ROPE_BASE ** (-jnp.arange(half_dim, dtype=jnp.float32) * 2.0 / tensor.shape[-1])
    angles = positions.astype(jnp.float32)[:, None] * frequency[None, :]
    cosine = jnp.cos(angles)[:, None, :]
    sines = jnp.sin(angles)[:, None, :]
    front_half = tensor[..., :half_dim]
    second = tensor[..., half_dim:]
    return jnp.concatenate(
        [front_half * cosine - second * sines, second * cosine + front_half * sines], axis=-1
    )


def doc_layout(lengths, row_ids):
    doc_ends = jnp.cumsum(lengths)
    before = row_ids[:, None] >= doc_ends[None, :]
    doc_ids = jnp.sum(before.astype(jnp.int32), axis=1)
    doc_start = jnp.sum(jnp.where(before, lengths[None, :], 0), axis=1)
    return (doc_ids, row_ids - doc_start)


def relayout(tokens, context_row, this_dev, devices):
    rows_dev, feature_width = tokens.shape
    cap_rows = 3 * rows_dev // (2 * devices)
    peer_ids = jnp.arange(devices, dtype=jnp.int32)
    own_rows = lax.dynamic_slice_in_dim(context_row, this_dev * rows_dev, rows_dev)
    target = own_rows // rows_dev
    onehot = (target[:, None] == peer_ids[None, :]).astype(jnp.int32)
    rank_in = jnp.sum(jnp.cumsum(onehot, axis=0) * onehot, axis=1) - 1
    outgoing = (
        jnp.zeros((devices * cap_rows, feature_width), tokens.dtype)
        .at[target * cap_rows + rank_in]
        .set(tokens)
    )
    arrived = lax.all_to_all(
        outgoing.reshape(devices, cap_rows, feature_width),
        "ctx",
        split_axis=0,
        concat_axis=0,
        tiled=True,
    )
    row_table = context_row.reshape(devices, rows_dev)
    is_here = row_table // rows_dev == this_dev
    arrival = jnp.cumsum(is_here.astype(jnp.int32), axis=1) - 1
    slot_idx = jnp.where(is_here, arrival, cap_rows)
    landing = (
        jnp.full((devices, cap_rows + 1), rows_dev, jnp.int32)
        .at[peer_ids[:, None], slot_idx]
        .set(row_table % rows_dev)
    )
    landing = landing[:, :cap_rows].reshape(-1)
    return (
        jnp.zeros((rows_dev, feature_width), tokens.dtype)
        .at[landing]
        .set(arrived.reshape(-1, feature_width), mode="drop")
    )


def per_device(tokens, context_row, lengths, q_weight, k_weight, v_weight, o_weight):
    devices = lax.axis_size("ctx")
    this_dev = lax.axis_index("ctx")
    rows_dev = tokens.shape[0]
    placed = relayout(tokens, context_row, this_dev, devices)
    gathered = lax.all_gather(placed, "head", axis=1, tiled=True)
    row_ids = this_dev * rows_dev + jnp.arange(rows_dev, dtype=jnp.int32)
    doc_ids, position = doc_layout(lengths, row_ids)

    def add_rows(segments):
        return tuple(
            (jnp.dot(gathered, segment, preferred_element_type=jnp.float32) for segment in segments)
        )

    q_raw = add_rows((lax.all_gather(q_weight, "ctx", axis=0, tiled=True),))[0]
    k_raw, v_raw = add_rows(
        (
            lax.all_gather(k_weight, "ctx", axis=0, tiled=True),
            lax.all_gather(v_weight, "ctx", axis=0, tiled=True),
        )
    )
    q_heads = rotate(q_raw.reshape(rows_dev, -1, HD), position).astype(jnp.bfloat16)
    key_rows = rotate(k_raw.reshape(rows_dev, -1, HD), position).astype(jnp.bfloat16)
    value_rows = v_raw.astype(jnp.bfloat16).reshape(rows_dev, -1, HD)
    stacked = jnp.stack([key_rows, value_rows])
    blocks = [stacked]
    carried = stacked
    for distance in range(REACH):
        carried = shifted(carried, "ctx", 1)
        blocks.append(carried)
    allowed_list = []
    needed = []
    for distance in range(len(blocks)):
        key_ids = row_ids - distance * rows_dev
        key_docs = jnp.where(key_ids >= 0, doc_layout(lengths, key_ids)[0], -1)
        allowed = (key_docs[None, :] == doc_ids[:, None]) & (key_ids[None, :] <= row_ids[:, None])
        allowed_list.append(allowed)
        needed.append(jnp.any(allowed))
    every_block = jnp.stack(blocks)
    key_stack = jnp.transpose(every_block[:, 0], (2, 0, 1, 3))
    value_stack = jnp.transpose(every_block[:, 1], (2, 0, 1, 3))
    group_size = HEADS // KV_HEADS
    factor = 1.0 / math.sqrt(HD)
    q_major = jnp.transpose(q_heads, (1, 0, 2))
    kv_owner = jnp.arange(q_major.shape[0], dtype=jnp.int32) // group_size

    def one_head(operands):
        query_head, head_index = operands
        key_set = key_stack[head_index]
        value_set = value_stack[head_index]
        scores = []
        for block in range(len(blocks)):

            def compute(block=block):
                raw_scores = (
                    jnp.einsum(
                        "qd,kd->qk", query_head, key_set[block], preferred_element_type=jnp.float32
                    )
                    * factor
                )
                return jnp.where(allowed_list[block], raw_scores, -jnp.inf)

            scores.append(compute())
        row_top = jnp.max(
            jnp.stack([jnp.max(block_scores, axis=1) for block_scores in scores]), axis=0
        )
        denominator = jnp.zeros((rows_dev,), jnp.float32)
        summed = jnp.zeros((rows_dev, HD), jnp.float32)
        for block in range(len(blocks)):
            weighting = jnp.exp(scores[block] - row_top[:, None])
            denominator = denominator + jnp.sum(weighting, axis=1)
            weights = weighting.astype(jnp.bfloat16)

            def product(weights=weights, block=block):
                return jnp.dot(weights, value_set[block], preferred_element_type=jnp.float32)

            summed = summed + product()
        return (summed / denominator[:, None]).astype(jnp.bfloat16)

    head_out = lax.map(one_head, (q_major, kv_owner))
    attended = jnp.transpose(head_out, (1, 0, 2)).reshape(rows_dev, -1)
    partial_out = jnp.dot(
        attended,
        lax.all_gather(o_weight, "ctx", axis=1, tiled=True),
        preferred_element_type=jnp.float32,
    ).astype(jnp.bfloat16)
    return (
        lax.psum_scatter(partial_out, "head", scatter_dimension=1, tiled=True)
        .astype(jnp.float32)
        .astype(jnp.bfloat16)
    )


def solution(mesh):
    return jax.shard_map(
        per_device,
        mesh=mesh,
        in_specs=(
            P("ctx", "head"),
            P(),
            P(),
            P("ctx", "head"),
            P("ctx", "head"),
            P("ctx", "head"),
            P("head", "ctx"),
        ),
        out_specs=P("ctx", "head"),
        check_vma=False,
    )
```

profile of v0, /device:TPU:5, one launch (start us, length us, event | category | flops | bytes accessed | tf_op | source)
XLA Modules:
  0.0 396.9 jit_solution(15614594111117597200)
XLA Ops:
  6.5 0.7 all-gather.10.cloned.1.call-update
  7.3 0.8 and_select_fusion
  8.5 0.8 compare_select_fusion.3
  9.3 1.7 scatter_custom_fusion
  10.9 1.1 reshape.432
  12.0 12.3 %all-to-all-start = ((bf16[64,3,1024]{2,1,0:T(4,128)(2,1)}), bf16[64,3,1024]{2,1,0:T(4,128)(2,1)S(1)}, u32[]{:S(2)}, u32[]{:S(2)}) async-start(bf16[64,3,1024]{2,1,0:T(4,128)(2,1)} %reshape.432), calls=%async_computation | async-start | bytes 1048576 | tf_op jit(solution)/shard_map/all_to_all | solution.py:57
  24.4 0.8 fusion.87
  25.2 4.4 %copy.80 = s32[64,128,1]{2,0,1:T(8,128)} copy(s32[64,128,1]{1,0,2:T(8,128)S(1)} %get-tuple-element.291) | data formatting | bytes 65536 | tf_op jit(solution)/shard_map/convert_element_type | solution.py:66
  29.7 4.5 %fusion.94 = s32[64,128,1]{2,0,1:T(8,128)} fusion(s32[64,128,1]{2,0,1:T(8,128)} %copy.80), kind=kOutput, calls=%fused_computation.154 | output fusion | flops 1040384 | bytes 65536 | tf_op jit(solution)/shard_map/jit(cumsum)/reduce_window_sum | solution.py:66
  34.2 3.7 copy.81
  38.5 30.4 %scatter_custom_fusion.2 = s32[256]{0:T(256)S(1)} fusion(s32[8192]{0:T(1024)S(1)} %bitcast.144, s32[8192]{0:T(1024)S(1)} %fusion.79, s32[]{:T(128)} %constant.119.clone.1), kind=kCustom, calls=%fused_computation.139 | custom fusion | bytes 1028
  69.6 2.1 scatter_custom_fusion.1
  71.7 0.7 all-gather.12.cloned.1.call-update
  72.5 0.5 all-gather.8.cloned.1.call-update
  73.0 0.5 all-gather.14.cloned.1.call-update
  74.3 16.4 %all-gather.10.cloned.1.call-done = bf16[4096,128]{1,0:T(8,128)(2,1)} async-done(((bf16[64,128]{1,0:T(8,128)(2,1)}), bf16[4096,128]{1,0:T(8,128)(2,1)}) %all-gather.10.cloned.1.call-update) | async-done | bytes 1048592 | tf_op jit(solution)/shard_map/all_gather | solution.py:98
  90.7 23.8 %all-gather.6.cloned.1.call-done = bf16[128,4096]{1,0:T(8,128)(2,1)} async-done(((bf16[128,1024]{1,0:T(8,128)(2,1)}), bf16[128,4096]{1,0:T(8,128)(2,1)}) %all-gather.6.cloned.1.call-update) | async-done | bytes 1048592 | tf_op jit(solution)/shard_map/all_gather | solution.py:86
  114.6 2.1 convolution_bitcast_fusion.1
  116.8 79.5 %all-gather.12.cloned.1.call-done = bf16[4096,128]{1,0:T(8,128)(2,1)} async-done(((bf16[64,128]{1,0:T(8,128)(2,1)}), bf16[4096,128]{1,0:T(8,128)(2,1)}) %all-gather.12.cloned.1.call-update) | async-done | bytes 1048592 | tf_op jit(solution)/shard_map/all_gather | solution.py:99
  196.3 2.1 fusion.60
  198.4 2.3 collective-permute-start
  201.0 1.0 collective-permute-done
  202.0 4.3 %collective-permute-start.1 = (bf16[2,128,1,128]{1,3,2,0:T(8,128)(2,1)S(1)}, bf16[2,128,1,128]{1,3,2,0:T(8,128)(2,1)S(1)}, u32[]{:S(2)}, u32[]{:S(2)}) collective-permute-start(bf16[2,128,1,128]{1,3,2,0:T(8,128)(2,1)S(1)} %collective-permute-done), channel_id=1, source_target_pairs={{0,4},{4,8},{8,12},{12,16},{16,20},{20,24},{24,28},{28,32},{32,36}... | collective-permute-start | bytes 196616 | tf_op jit(solution)/shard_map/ppermute | solution.py:20
  206.3 1.3 collective-permute-done.1
  207.6 4.4 %collective-permute-start.2 = (bf16[2,128,1,128]{1,3,2,0:T(8,128)(2,1)S(1)}, bf16[2,128,1,128]{1,3,2,0:T(8,128)(2,1)S(1)}, u32[]{:S(2)}, u32[]{:S(2)}) collective-permute-start(bf16[2,128,1,128]{1,3,2,0:T(8,128)(2,1)S(1)} %collective-permute-done.1), channel_id=1, source_target_pairs={{0,4},{4,8},{8,12},{12,16},{16,20},{20,24},{24,28},{28,32},{32,36}... | collective-permute-start | bytes 196616 | tf_op jit(solution)/shard_map/ppermute | solution.py:20
  212.0 1.1 collective-permute-done.2
  213.5 66.2 %all-gather.8.cloned.1.call-done = bf16[4096,1024]{1,0:T(8,128)(2,1)} async-done(((bf16[64,1024]{1,0:T(8,128)(2,1)}), bf16[4096,1024]{1,0:T(8,128)(2,1)}) %all-gather.8.cloned.1.call-update) | async-done | bytes 8388624 | tf_op jit(solution)/shard_map/all_gather | solution.py:95
  279.7 5.0 %convolution_bitcast_fusion = f32[16,8,8,128]{3,1,2,0:T(8,128)S(1)} fusion(bf16[128,4096]{1,0:T(8,128)(2,1)} %all-gather.6.cloned.1.call-done, bf16[4096,1024]{1,0:T(8,128)(2,1)} %all-gather.8.cloned.1.call-done), kind=kOutput, calls=%fused_computation.70 | convolution fusion | flops 1073741824 | bytes 9961472 | tf_op jit(solution)/shard_map/dot_general | solution.py:92
  285.3 14.4 %while.13 = (s32[]{:T(128)}, bf16[8,128,128]{1,2,0:T(8,128)(2,1)S(1)}, bf16[8,128,128]{2,1,0:T(8,128)(2,1)S(1)}, bf16[1,4,128,128]{3,2,1,0:T(8,128)(2,1)S(1)}, b...) while((s32[]{:T(128)}, ...), condition=%wide.region_21.22_spmd.clone.clone, body=%wide.region_12.21_spmd.clone.clone.sunk | while | flops 34291456 | bytes 1757353 | solution.py:160
  299.7 62.8 %all-gather.14.cloned.1.call-done = bf16[1024,4096]{0,1:T(8,128)(2,1)} async-done(((bf16[1024,64]{0,1:T(8,128)(2,1)}), bf16[1024,4096]{0,1:T(8,128)(2,1)}) %all-gather.14.cloned.1.call-update) | async-done | bytes 8388624 | tf_op jit(solution)/shard_map/all_gather | solution.py:164
  362.5 7.4 %convolution_convert_fusion = bf16[128,4096]{1,0:T(8,128)(2,1)} fusion(bf16[128,1024]{0,1:T(8,128)(2,1)S(1)} %bitcast.140, bf16[1024,4096]{0,1:T(8,128)(2,1)} %all-gather.14.cloned.1.call-done), kind=kOutput, calls=%fused_computation.69 | convolution fusion | flops 1074266112 | bytes 9699328 | tf_op jit(solution)/shard_map/dot_general | solution.py:162
  369.9 20.2 %reduce-scatter.2.cloned.1.call-done = bf16[128,1024]{1,0:T(8,128)(2,1)} async-done(((bf16[128,4096]{1,0:T(8,128)(2,1)}), bf16[128,1024]{1,0:T(8,128)(2,1)}) %reduce-scatter.2.cloned.1.call-update) | async-done | bytes 262160 | tf_op jit(solution)/shard_map/reduce_scatter | solution.py:168
  (162 shorter events, 17.8 us)
Async XLA Ops:
  6.5 84.2 %all-gather.10.cloned.1.call-start = ((), (), s32[]{:S(2)}) async-start(), calls=%async_computation.4 | async-start | bytes 1064960 | tf_op jit(solution)/shard_map/all_gather | solution.py:98
  12.0 57.2 %all-to-all-start = ((bf16[64,3,1024]{2,1,0:T(4,128)(2,1)}), bf16[64,3,1024]{2,1,0:T(4,128)(2,1)S(1)}, u32[]{:S(2)}, u32[]{:S(2)}) async-start(bf16[64,3,1024]{2,1,0:T(4,128)(2,1)} %reshape.432), calls=%async_computation | async-start | bytes 1048576 | tf_op jit(solution)/shard_map/all_to_all | solution.py:57
  24.3 90.2 %all-gather.6.cloned.1.call-start = ((), (), s32[]{:S(2)}) async-start(), calls=%async_computation.2 | async-start | bytes 1310720 | tf_op jit(solution)/shard_map/all_gather | solution.py:86
  25.2 12.8 %copy-start.3 = (s32[2]{0:T(128)S(1)}, s32[2]{0:T(128)}, u32[]{:S(2)}) copy-start(s32[2]{0:T(128)} %constant.138) | copy-start | bytes 28
  25.2 13.0 %copy-start.2 = (s32[2]{0:T(128)S(1)}, s32[2]{0:T(128)}, u32[]{:S(2)}) copy-start(s32[2]{0:T(128)} %constant.135) | copy-start | bytes 28
  25.2 13.2 %copy-start = (s32[8192]{0:T(1024)S(1)}, s32[8192]{0:T(1024)}, u32[]{:S(2)}) copy-start(s32[8192]{0:T(1024)} %param.10) | copy-start | bytes 98308
  29.7 44.0 %copy-start.1 = (s32[64]{0:T(128)S(1)}, s32[64]{0:T(128)}, u32[]{:S(2)}) copy-start(s32[64]{0:T(128)} %param.11) | copy-start | bytes 772
  71.7 124.6 %all-gather.12.cloned.1.call-start = ((), (), s32[]{:S(2)}) async-start(), calls=%async_computation.5 | async-start | bytes 1064960 | tf_op jit(solution)/shard_map/all_gather | solution.py:99
  72.4 207.3 %all-gather.8.cloned.1.call-start = ((), (), s32[]{:S(2)}) async-start(), calls=%async_computation.3 | async-start | bytes 8519680 | tf_op jit(solution)/shard_map/all_gather | solution.py:95
  73.0 289.5 %all-gather.14.cloned.1.call-start = ((), (), s32[]{:S(2)}) async-start(), calls=%async_computation.6 | async-start | bytes 8519680 | tf_op jit(solution)/shard_map/all_gather | solution.py:164
  73.6 316.5 %reduce-scatter.2.cloned.1.call-start = ((), (), s32[]{:S(2)}) async-start(), calls=%async_computation.7 | async-start | bytes 1310720 | tf_op jit(solution)/shard_map/reduce_scatter | solution.py:168
  198.4 3.6 collective-permute-start
  202.0 5.6 %collective-permute-start.1 = (bf16[2,128,1,128]{1,3,2,0:T(8,128)(2,1)S(1)}, bf16[2,128,1,128]{1,3,2,0:T(8,128)(2,1)S(1)}, u32[]{:S(2)}, u32[]{:S(2)}) collective-permute-start(bf16[2,128,1,128]{1,3,2,0:T(8,128)(2,1)S(1)} %collective-permute-done), channel_id=1, source_target_pairs={{0,4},{4,8},{8,12},{12,16},{16,20},{20,24},{24,28},{28,32},{32,36}... | collective-permute-start | bytes 196616 | tf_op jit(solution)/shard_map/ppermute | solution.py:20
  207.6 5.6 %collective-permute-start.2 = (bf16[2,128,1,128]{1,3,2,0:T(8,128)(2,1)S(1)}, bf16[2,128,1,128]{1,3,2,0:T(8,128)(2,1)S(1)}, u32[]{:S(2)}, u32[]{:S(2)}) collective-permute-start(bf16[2,128,1,128]{1,3,2,0:T(8,128)(2,1)S(1)} %collective-permute-done.1), channel_id=1, source_target_pairs={{0,4},{4,8},{8,12},{12,16},{16,20},{20,24},{24,28},{28,32},{32,36}... | collective-permute-start | bytes 196616 | tf_op jit(solution)/shard_map/ppermute | solution.py:20
Sparse Core Ops, SparseCore 0:
  10.1 80.5 all-gather.9
  92.5 21.9 all-gather.5
  117.3 78.9 all-gather.11
  198.9 80.7 all-gather.7
  282.3 80.1 all-gather.13
  370.0 20.0 reduce-scatter.1
where the time goes:
time: 400 us; the launch traced here: 397 us
  waiting for transfers between devices  275 us (69%)
  local copies, waits for them, and re-layouts  46.1 us (12%)
  matrix products  28.7 us (7%)
  starting transfers between devices  23.5 us (6%)
  between operations  13.8 us (3%)
  other arithmetic  9.56 us (2%)
    all_gather x1, waiting for transfers between devices, per_device(): lax.all_gather(v_weight, 'ctx', axis=0, tiled=True)  79.5 us
    all_gather x1, waiting for transfers between devices, per_device(): q_raw = add_rows((lax.all_gather(q_weight, 'ctx', axis=0, tiled=True),))[0]  66.2 us
    all_gather x1, waiting for transfers between devices, per_device(): lax.all_gather(o_weight, 'ctx', axis=1, tiled=True)  62.8 us
    unnamed x16, local copies, waits for them, and re-layouts  31.2 us
    all_gather x1, waiting for transfers between devices, per_device(): gathered = lax.all_gather(placed, 'head', axis=1, tiled=True)  23.8 us
    reduce_scatter x1, waiting for transfers between devices, per_device(): lax.psum_scatter(partial_out, 'head', scatter_dimension=1, tiled=True)  20.2 us
    all_gather x1, waiting for transfers between devices, per_device(): lax.all_gather(k_weight, 'ctx', axis=0, tiled=True)  16.4 us
    all_to_all x1, starting transfers between devices, relayout(): lax.all_to_all(outgoing.reshape(devices, cap_rows, feature_width), 'ctx',...  12.3 us
  transfers between devices with their start and end apart: 10, of which 9 were waited for; matrix products, arithmetic and copies ran while one was open for 19% of the time, Pallas kernels for 0%

commit v1 on v0

v1 whole, which is shorter than its diff:
```python
import math

import jax
import jax.numpy as jnp
from jax import lax
from jax.experimental import pallas as pl
from jax.experimental.pallas import tpu as pltpu
from jax.sharding import PartitionSpec as P

MESH = pl.DeviceIdType.MESH
F32 = jnp.float32
BF16 = jnp.bfloat16
ROPE_BASE = 500000.0
HD = 128

DZ = (0, 1, -1, 2, -2, 3, -3, 4)
DY = (0, 1, -1, 2)
ZS = {d: i for i, d in enumerate(DZ)}
YS = {d: i for i, d in enumerate(DY)}
GROUPS = ((0, 1), (1, 3), (3, 5), (5, 7), (7, 8))

LINK_RATE, LINK_LATENCY = 47.0, 2.0
PEER_RATE, PEER_LATENCY = 400.0, 1.0


class Message:
    def __init__(self, name, link, src, dst, deps, size, prio):
        self.name, self.link, self.src, self.dst = name, link, src, dst
        self.deps, self.size, self.prio = deps, size, prio


def gather_messages(tag, rows, width1, width2, ready, rank):
    out = []
    half = rows // 2
    size1 = rows * width1 * 2e-3
    size2 = rows * width2 * 2e-3
    full, top, bottom = (0, rows), (0, half), (half, half)

    def one(dz, dy, part):
        return (tag + "1", ZS[dz], YS[dy], part)

    def pair(dz, which):
        return (tag + "1", ZS[dz], (2 * which, 2), full)

    def two(dy, dz, part):
        return (tag + "2", YS[dy], ZS[dz], part)

    def group(dy, g):
        lo, hi = GROUPS[g]
        return (tag + "2", YS[dy], (lo, hi - lo), full)

    def add(name, link, src, dst, deps, size, prio):
        out.append(Message(tag + name, link, src, dst, [tag + d for d in deps] + ready, size, (rank,) + prio))

    add("1y+1", "+y", one(0, 0, full), one(0, -1, full), [], size1, (0, 1))
    add("1y-1", "-y", one(0, 0, full), one(0, 1, full), [], size1, (0, 1))
    add("1y+2", "+y", one(0, -1, top), one(0, 2, top), ["1y+1"], size1 / 2, (0, 2))
    add("1y-2", "-y", one(0, 1, bottom), one(0, 2, bottom), ["1y-1"], size1 / 2, (0, 2))
    first = {0: ["1y-1"], 1: ["1y+1", "1y+2", "1y-2"]}
    for which in (0, 1):
        for sign, link in ((1, "+z"), (-1, "-z")):
            mark = "+" if sign > 0 else "-"
            for step in (1, 2, 3, 4):
                if step == 4 and (sign > 0) != (which == 0):
                    continue
                deps = first[which] if step == 1 else [f"1z{which}{mark}{step - 1}"]
                far = 4 if step == 4 else -sign * step
                add(f"1z{which}{mark}{step}", link, pair(-sign * (step - 1), which), pair(far, which), deps,
                    2 * size1, (1, step))
    for sign, link in ((1, "+z"), (-1, "-z")):
        mark = "+" if sign > 0 else "-"
        for step in (1, 2, 3, 4):
            deps = [] if step == 1 else [f"2z{mark}{step - 1}"]
            part = full if step < 4 else (top if sign > 0 else bottom)
            far = 4 if step == 4 else -sign * step
            add(f"2z{mark}{step}", link, two(0, -sign * (step - 1), part), two(0, far, part), deps,
                size2 if step < 4 else size2 / 2, (0, step))
    for g, (lo, hi) in enumerate(GROUPS):
        deps = [] if g == 0 else [f"2z+{g}", f"2z-{g}"]
        amount = size2 * (hi - lo)
        add(f"2y{g}+1", "+y", group(0, g), group(-1, g), deps, amount, (1, g))
        add(f"2y{g}-1", "-y", group(0, g), group(1, g), deps, amount, (1, g))
        if g % 2 == 0:
            add(f"2y{g}+2", "+y", group(-1, g), group(2, g), [f"2y{g}+1"], amount, (1, g))
        else:
            add(f"2y{g}-2", "-y", group(1, g), group(2, g), [f"2y{g}-1"], amount, (1, g))
    return out


def needs(tag, dz):
    g = [i for i, (lo, hi) in enumerate(GROUPS) if lo <= ZS[dz] < hi][0]
    far = f"2y{g}+2" if g % 2 == 0 else f"2y{g}-2"
    names = [f"2y{g}+1", f"2y{g}-1", far]
    if dz == 0:
        names += ["1y+1", "1y-1", "1y+2", "1y-2"]
    elif dz == 4:
        names += ["1z0+4", "1z1-4", "2z+4", "2z-4"]
    else:
        mark, step = ("+" if dz < 0 else "-"), abs(dz)
        names += [f"1z0{mark}{step}", f"1z1{mark}{step}", f"2z{mark}{step}"]
    return [tag + n for n in names]


def all_messages():
    out = [
        Message("w1", "peer", None, None, [], 33, (0,)),
        Message("w2", "peer", None, None, [], 50, (0,)),
        Message("xs", "peer", None, None, [], 262, (0,)),
        Message("x+", "+x", None, None, [], 262, (0,)),
        Message("x-", "-x", None, None, [], 262, (0,)),
        Message("x+2", "+x", None, None, ["x+"], 131, (1,)),
        Message("x-2", "-x", None, None, ["x-"], 131, (1,)),
        Message("xs+", "peer", None, None, ["x+"], 262, (1,)),
        Message("xs-", "peer", None, None, ["x-"], 262, (1,)),
        Message("xs2", "peer", None, None, ["x+2", "x-2"], 262, (1,)),
    ]
    out += gather_messages("q", 128, 256, 384, ["w1", "w2"], 0)
    out += gather_messages("o", 64, 384, 640, [], 1)
    return out


def simulate(messages):
    free, arrival, start = {}, {}, {}
    pending = list(messages)
    while pending:
        best = None
        by_link = {}
        for m in pending:
            if all(d in arrival for d in m.deps):
                at = max([arrival[d] for d in m.deps], default=0.0)
                by_link.setdefault(m.link, []).append((at, m))
        for link, options in by_link.items():
            begin = max(free.get(link, 0.0), min(at for at, _ in options))
            at, m = min(((at, m) for at, m in options if at <= begin), key=lambda p: p[1].prio)
            if best is None or begin < best[0]:
                best = (begin, m, at)
        begin, m, at = best
        peer = m.link == "peer"
        span = m.size / (PEER_RATE if peer else LINK_RATE)
        free[m.link] = begin + span
        arrival[m.name] = begin + span + (PEER_LATENCY if peer else LINK_LATENCY)
        start[m.name] = max(at, begin - 3.0)
        pending.remove(m)
    return start, arrival


HALO = ["halo"]
ATTEND = [f"att{qb}{pair}" for qb in (0, 1) for pair in (0, 1)]


def steps_of():
    x_all = ["x+", "x-", "xs", "xs+", "xs-", "xs2"]
    steps = [("tables", [], 1.5)]
    steps += [(f"q{dz}", needs("q", dz) + x_all + ["tables"], 0.6) for dz in DZ]
    steps += [("kv", [f"q{dz}" for dz in DZ], 0.5), ("rope", ["kv"], 1.0), ("halo", ["kv"], 0.5)]
    steps += [(name, ["halo", "rope"], 1.0) for name in ATTEND]
    steps += [("attsend0", ATTEND[:2], 0.1), ("attsend1", ATTEND[2:], 0.1)]
    steps += [("attget", ["attsend0", "attsend1"], 0.1)]
    steps += [(f"o{dz}", needs("o", dz) + ["attget"], 0.5) for dz in DZ]
    return steps


def plan():
    messages = all_messages()
    start, arrival = simulate(messages)
    actions = [(start[m.name], 1, "send", m.name) for m in messages]
    actions += [(arrival[m.name], 0, "recv", m.name) for m in messages]
    actions.sort()
    steps = steps_of()
    halo_from = {"halo": 4.0, "attget": 1.0}
    done, finished, order, clock = set(), {}, [], 0.0
    waiting = list(steps)
    index = 0
    while index < len(actions) or waiting:
        ready = None
        for step in waiting:
            if all(d in done for d in step[1]):
                late = max([finished.get(d, 0.0) for d in step[1]], default=0.0) + halo_from.get(step[0], 0.0)
                if index >= len(actions) or max(clock, late) <= actions[index][0] - 0.1:
                    ready = (step, late)
                    break
        if ready is not None:
            step, late = ready
            order.append(("step", step[0]))
            clock = max(clock, late) + step[2]
            finished[step[0]] = clock
            done.add(step[0])
            waiting.remove(step)
            continue
        at, _, kind, name = actions[index]
        index += 1
        order.append((kind, name))
        clock = max(clock, at) + 0.1
        if kind == "recv":
            done.add(name)
    return messages, order, max(arrival.values())


def kernel(messages, order, placed, lens, qw, kw, vw, ow, out,
           q1, q2, o1, o2, st1, st2, xs, acc1, acc2, cs, bias, qs, kv, vt, att, part, rs,
           send, recv, hsend, hrecv, asend, arecv, psend, precv):
    ctx, x = lax.axis_index("ctx"), lax.axis_index("head")
    z, y, core = ctx // 8, (ctx // 2) % 4, ctx % 2
    chip = ctx // 2
    other = 1 - core
    buffers = {"q1": q1, "q2": q2, "o1": o1, "o2": o2}
    number = {m.name: i for i, m in enumerate(messages)}

    def at(dz, dy, which, dx=0):
        return ((lax.rem(z + dz + 8, 8) * 4 + lax.rem(y + dy + 4, 4)) * 2 + which, lax.rem(x + dx + 4, 4))

    def chip_at(by, which):
        return (lax.rem(chip + by + 32, 32) * 2 + which, x)

    peers = [at(1, 0, core), at(-1, 0, core), at(0, 1, core), at(0, -1, core), at(0, 0, other)]
    peers += [at(0, 0, which, dx) for dx in (1, 2, 3) for which in (0, 1)]
    peers += [chip_at(by, which) for by in (1, 2, -1, -2) for which in (0, 1)]
    barrier = pltpu.get_barrier_semaphore()
    for peer in peers:
        pl.semaphore_signal(barrier, inc=1, device_id=peer, device_id_type=MESH)

    for d in (0, 1):
        st1[d] = qw[:, 512 * d : 512 * d + 256]
        st2[d, :, :256] = qw[:, 512 * d + 256 : 512 * d + 512]
        st2[d, :, 256:] = (kw if d == 0 else vw)[...]
    mine = pl.ds(pl.multiple_of(core * 64, 64), 64)
    theirs = pl.ds(pl.multiple_of(other * 64, 64), 64)
    q1[0, 0, mine] = st1[core]
    q2[0, 0, mine] = st2[core]
    xs[x, core] = placed[...]
    eye = (
        lax.broadcasted_iota(jnp.int32, (64, 64), 0) == lax.broadcasted_iota(jnp.int32, (64, 64), 1)
    ).astype(F32).astype(BF16)
    turned = lax.dot_general(eye, ow[...], (((1,), (1,)), ((), ())), preferred_element_type=F32).astype(BF16)
    o1[0, 0] = turned[:, :384]
    o2[0, 0] = turned[:, 384:]
    pl.semaphore_wait(barrier, len(peers))

    x_low, x_high, x_far = lax.rem(x + 3, 4), lax.rem(x + 1, 4), lax.rem(x + 2, 4)
    top, bottom = pl.ds(0, 64), pl.ds(64, 64)
    across = at(0, 0, other)
    special = {
        "w1": (st1.at[other], q1.at[0, 0, mine], q1.at[0, 0, theirs], across),
        "w2": (st2.at[other], q2.at[0, 0, mine], q2.at[0, 0, theirs], across),
        "xs": (xs.at[x, core], xs.at[x, core], xs.at[x, other], across),
        "x+": (xs.at[x, core], xs.at[x, core], xs.at[x_low, core], at(0, 0, core, 1)),
        "x-": (xs.at[x, core], xs.at[x, core], xs.at[x_high, core], at(0, 0, core, -1)),
        "x+2": (xs.at[x_low, core, top], xs.at[x_low, core, top], xs.at[x_far, core, top], at(0, 0, core, 1)),
        "x-2": (xs.at[x_high, core, bottom], xs.at[x_high, core, bottom], xs.at[x_far, core, bottom],
                at(0, 0, core, -1)),
        "xs+": (xs.at[x_low, core], xs.at[x_low, core], xs.at[x_low, other], across),
        "xs-": (xs.at[x_high, core], xs.at[x_high, core], xs.at[x_high, other], across),
        "xs2": (xs.at[x_far, core], xs.at[x_far, core], xs.at[x_far, other], across),
    }
    to = {"+z": at(1, 0, core), "-z": at(-1, 0, core), "+y": at(0, 1, core), "-y": at(0, -1, core)}

    def view(place):
        name, a, b, (lo, n) = place
        b = pl.ds(*b) if isinstance(b, tuple) else b
        return buffers[name].at[a, b, pl.ds(lo, n)]

    def remote(src, dst, ssem, rsem, device):
        return pltpu.make_async_remote_copy(
            src_ref=src, dst_ref=dst, send_sem=ssem, recv_sem=rsem, device_id=device, device_id_type=MESH
        )

    def copy_of(m, coming=False):
        i = number[m.name]
        if m.name in special:
            src, dst, land, device = special[m.name]
        else:
            src, dst, land, device = view(m.src), view(m.dst), view(m.dst), to[m.link]
        if coming:
            src = dst = land
        return remote(src, dst, send.at[i], recv.at[i], device)

    by_name = {m.name: m for m in messages}

    def tables():
        base = chip * 256
        i0 = lax.broadcasted_iota(jnp.int32, (64, 64), 0)
        i1 = lax.broadcasted_iota(jnp.int32, (64, 64), 1)
        spread = jnp.broadcast_to(lens[...].astype(F32), (64, 64))
        end_col = jnp.sum(jnp.where(i1 <= i0, spread, 0.0), axis=1, keepdims=True)
        len_col = jnp.sum(jnp.where(i1 == i0, spread, 0.0), axis=1, keepdims=True)
        end_row = jnp.sum(jnp.where(i0 <= i1, jnp.broadcast_to(len_col, (64, 64)), 0.0), axis=0, keepdims=True)
        row_id = (base + lax.broadcasted_iota(jnp.int32, (64, 256), 1)).astype(F32)
        before = row_id >= end_col
        q_doc = jnp.sum(jnp.where(before, 1.0, 0.0), axis=0, keepdims=True)
        position = row_id - jnp.sum(jnp.where(before, len_col, 0.0), axis=0, keepdims=True)
        turn = lax.broadcasted_iota(jnp.int32, (64, 256), 0).astype(F32)
        angle = position * jnp.exp(turn * (-2.0 / HD * math.log(ROPE_BASE)))
        cs[...] = jnp.transpose(jnp.concatenate([jnp.cos(angle), jnp.sin(angle)], axis=0))
        key_id = base - 384 + lax.broadcasted_iota(jnp.int32, (640, 64), 0)
        k_doc = jnp.sum(jnp.where(key_id.astype(F32) >= end_row, 1.0, 0.0), axis=1, keepdims=True)
        for qb in (0, 1):
            lo = 128 * qb
            kid = base - 384 + lo + lax.broadcasted_iota(jnp.int32, (512, 128), 0)
            qid = base + lo + lax.broadcasted_iota(jnp.int32, (512, 128), 1)
            allowed = (k_doc[lo : lo + 512] == q_doc[:, lo : lo + 128]) & (kid <= qid) & (kid >= 0)
            bias[qb] = jnp.where(allowed, 0.0, -jnp.inf)

    def columns_of(dz):
        zz = lax.rem(z + dz + 8, 8)
        parts = []
        for dy in DY:
            lane = pl.multiple_of((lax.rem(zz, 2) * 4 + lax.rem(y + dy + 4, 4)) * 128, 128)
            parts.append(xs[zz // 2, :, :, pl.ds(lane, 128)].reshape(256, 128))
        return jnp.concatenate(parts, axis=1)

    def project(dz):
        s = ZS[dz]
        lhs = columns_of(dz)
        one = jnp.dot(lhs, q1[s].reshape(512, 256), preferred_element_type=F32)
        two = jnp.dot(lhs, q2[:, s].reshape(512, 384), preferred_element_type=F32)
        if dz == 0:
            acc1[...] = one
            acc2[...] = two
        else:
            acc1[...] += one
            acc2[...] += two

    def turned_pairs():
        table = cs[...]
        swapped = pltpu.roll(table, 64, 1)
        low = lax.broadcasted_iota(jnp.int32, (256, 128), 1) < 64
        return jnp.where(low, table, swapped), jnp.where(low, -swapped, table)

    def rope(e):
        cosine, sine = turned_pairs()
        return e * cosine + pltpu.roll(e, 64, 1) * sine

    halo = [
        (0, core, pl.ds(384, 256), pl.ds(384, 256), across),
        (1, 0, pl.ds(384, 256), pl.ds(128, 256), chip_at(1, 0)),
        (2, 0, pl.ds(384, 256), pl.ds(128, 256), chip_at(1, 1)),
        (3, 0, pl.ds(512, 128), pl.ds(0, 128), chip_at(2, 0)),
        (4, 0, pl.ds(512, 128), pl.ds(0, 128), chip_at(2, 1)),
    ]

    def halo_copy(i):
        kind, _, src, dst, device = halo[i]
        return remote(kv.at[core, src], kv.at[core, dst], hsend.at[i], hrecv.at[core, (kind + 1) // 2], device)

    def make_kv():
        raw = acc2[:, 256:384]
        kv[core, 384:640] = jnp.where(core == 0, rope(raw), raw).astype(BF16)
        for i in range(5):
            halo_copy(i).start()

    def rope_queries():
        for h in range(4):
            e = acc1[:, 128 * h : 128 * h + 128] if h < 2 else acc2[:, 128 * (h - 2) : 128 * (h - 2) + 128]
            turned_e = rope(e).astype(BF16)
            for qb in (0, 1):
                qs[qb, h // 2, 128 * (h % 2) : 128 * (h % 2) + 128] = turned_e[128 * qb : 128 * qb + 128]

    def wait_halo():
        remote(kv.at[other, pl.ds(384, 256)], kv.at[other, pl.ds(384, 256)], hsend.at[0],
               hrecv.at[other, 0], across).wait_recv()
        for c in (0, 1):
            remote(kv.at[c, pl.ds(128, 256)], kv.at[c, pl.ds(128, 256)], hsend.at[1], hrecv.at[c, 1],
                   across).wait_recv()
            remote(kv.at[c, pl.ds(0, 128)], kv.at[c, pl.ds(0, 128)], hsend.at[3], hrecv.at[c, 2],
                   across).wait_recv()
        eye = (
            lax.broadcasted_iota(jnp.int32, (128, 128), 0) == lax.broadcasted_iota(jnp.int32, (128, 128), 1)
        ).astype(F32).astype(BF16)
        vt[...] = lax.dot_general(eye, kv[1], (((1,), (1,)), ((), ())), preferred_element_type=F32).astype(BF16)

    def attend(qb, pair):
        keys = kv[0, 128 * qb : 128 * qb + 512]
        scores = lax.dot_general(keys, qs[qb, pair], (((1,), (1,)), ((), ())), preferred_element_type=F32)
        mask = bias[qb]
        scores = scores * (1.0 / math.sqrt(HD)) + jnp.concatenate([mask, mask], axis=1)
        expo = jnp.exp(scores - jnp.max(scores, axis=0, keepdims=True))
        denominator = jnp.sum(expo, axis=0, keepdims=True)
        summed = jnp.dot(vt[:, 128 * qb : 128 * qb + 512], expo.astype(BF16), preferred_element_type=F32)
        result = (summed / denominator).astype(BF16)
        for h in (0, 1):
            att[core, qb, 128 * (2 * pair + h) : 128 * (2 * pair + h) + 128] = result[:, 128 * h : 128 * h + 128]

    def att_copy(qb):
        return remote(att.at[core, qb], att.at[core, qb], asend.at[qb], arecv.at[qb], across)

    def wait_att():
        for qb in (0, 1):
            remote(att.at[other, qb], att.at[other, qb], asend.at[qb], arecv.at[qb], across).wait_recv()

    def part_copy(dz, t, start):
        s = ZS[dz]
        zz = lax.rem(z + dz + 8, 8)
        goal = zz // 2
        here = (goal == x) & (core == t)
        sem = precv.at[core, x, lax.rem(zz, 2)]
        land = rs.at[core, x, lax.rem(zz, 2)]

        @pl.when(jnp.logical_not(here))
        def _():
            copy = remote(part.at[s, t], land, psend.at[s, t], sem, (chip * 2 + t, goal))
            copy.start() if start else copy.wait_send()

        if start:

            @pl.when(here)
            def _():
                pltpu.make_async_copy(part.at[s, t], land, sem).start()

    def out_project(dz):
        s = ZS[dz]
        weights = jnp.concatenate([att[:, 0].reshape(1024, 128), att[:, 1].reshape(1024, 128)], axis=1)
        total = jnp.dot(o1[s].reshape(256, 384), weights[:384], preferred_element_type=F32)
        total += jnp.dot(o2[:, s].reshape(256, 640), weights[384:], preferred_element_type=F32)
        total = total.astype(BF16)
        for t in (0, 1):
            part[s, t] = total[:, 128 * t : 128 * t + 128]
            part_copy(dz, t, True)

    def run(name):
        if name == "tables":
            tables()
        elif name == "kv":
            make_kv()
        elif name == "rope":
            rope_queries()
        elif name == "halo":
            wait_halo()
        elif name == "attget":
            wait_att()
        elif name.startswith("attsend"):
            att_copy(int(name[7])).start()
        elif name.startswith("att"):
            attend(int(name[3]), int(name[4]))
        elif name.startswith("q"):
            project(int(name[1:]))
        else:
            out_project(int(name[1:]))

    for kind, name in order:
        if kind == "send":
            copy_of(by_name[name]).start()
        elif kind == "recv":
            copy_of(by_name[name], True).wait_recv()
        else:
            run(name)

    for m in messages:
        copy_of(m).wait_send()
    for i in range(5):
        halo_copy(i).wait_send()
    for qb in (0, 1):
        att_copy(qb).wait_send()
    for dz in DZ:
        for t in (0, 1):
            part_copy(dz, t, False)
    for zz in (0, 1):
        sums = []
        for c in (0, 1):
            total = None
            for g in range(4):
                land = rs.at[c, g, zz]
                remote(land, land, psend.at[0, 0], precv.at[c, g, zz], across).wait_recv()
                term = rs[c, g, zz].astype(F32)
                total = term if total is None else total + term
            sums.append(total)
        for dy in DY:
            s = YS[dy]
            block = jnp.concatenate([sums[0][64 * s : 64 * s + 64], sums[1][64 * s : 64 * s + 64]], axis=0)
            lane = pl.multiple_of((zz * 4 + lax.rem(y + dy + 4, 4)) * 128, 128)
            out[:, pl.ds(lane, 128)] = jnp.transpose(block).astype(BF16)


def fused(placed, lengths, qw, kw, vw, ow):
    messages, order, _ = plan()
    count = len(messages)
    dma = pltpu.SemaphoreType.DMA
    scratch = [
        pltpu.VMEM((8, 4, 128, 256), BF16),
        pltpu.VMEM((4, 8, 128, 384), BF16),
        pltpu.VMEM((8, 4, 64, 384), BF16),
        pltpu.VMEM((4, 8, 64, 640), BF16),
        pltpu.VMEM((2, 64, 256), BF16),
        pltpu.VMEM((2, 64, 384), BF16),
        pltpu.VMEM((4, 2, 128, 1024), BF16),
        pltpu.VMEM((256, 256), F32),
        pltpu.VMEM((256, 384), F32),
        pltpu.VMEM((256, 128), F32),
        pltpu.VMEM((2, 512, 128), F32),
        pltpu.VMEM((2, 2, 256, 128), BF16),
        pltpu.VMEM((2, 640, 128), BF16),
        pltpu.VMEM((128, 640), BF16),
        pltpu.VMEM((2, 2, 512, 128), BF16),
        pltpu.VMEM((8, 2, 256, 128), BF16),
        pltpu.VMEM((2, 4, 2, 256, 128), BF16),
        dma((count,)),
        dma((count,)),
        dma((5,)),
        dma((2, 3)),
        dma((2,)),
        dma((2,)),
        dma((8, 2)),
        dma((2, 4, 2)),
    ]

    def body(*refs):
        kernel(messages, order, *refs)

    return pl.pallas_call(
        body,
        out_shape=jax.ShapeDtypeStruct((128, 1024), BF16),
        in_specs=[pl.BlockSpec(memory_space=pltpu.VMEM)] * 6,
        out_specs=pl.BlockSpec(memory_space=pltpu.VMEM),
        scratch_shapes=scratch,
        compiler_params=pltpu.CompilerParams(
            collective_id=0, has_side_effects=True, vmem_limit_bytes=48 * 2**20
        ),
    )(placed, lengths.reshape(1, 64), qw, kw, vw, ow)


def relayout(tokens, context_row, this_dev, devices):
    rows_dev, width = tokens.shape
    cap = 3
    table = context_row.reshape(devices, rows_dev)
    own = lax.dynamic_slice_in_dim(context_row, this_dev * rows_dev, rows_dev)
    target = own // rows_dev
    row = jnp.arange(rows_dev, dtype=jnp.int32)
    rank = jnp.sum((target[:, None] == target[None, :]) & (row[None, :] < row[:, None]), axis=1, dtype=jnp.int32)
    slot = target * cap + rank
    pick = (jnp.arange(devices * cap, dtype=jnp.int32)[:, None] == slot[None, :]).astype(BF16)
    outgoing = jnp.dot(pick, tokens, preferred_element_type=F32).astype(BF16)
    arrived = lax.all_to_all(
        outgoing.reshape(devices, cap, width), "ctx", split_axis=0, concat_axis=0, tiled=True
    ).reshape(devices * cap, width)
    here = table // rows_dev == this_dev
    upper = (row[:, None] < row[None, :]).astype(BF16)
    order = jnp.dot(here.astype(BF16), upper, preferred_element_type=F32).astype(jnp.int32)
    landing = jnp.stack(
        [jnp.sum(jnp.where(here & (order == j), table % rows_dev + 1, 0), axis=1) - 1 for j in range(cap)], axis=1
    ).reshape(-1)
    place = (row[:, None] == landing[None, :]).astype(BF16)
    return jnp.dot(place, arrived, preferred_element_type=F32).astype(BF16)


def per_device(tokens, context_row, lengths, qw, kw, vw, ow):
    placed = relayout(tokens, context_row, lax.axis_index("ctx"), lax.axis_size("ctx"))
    return fused(placed, lengths, qw, kw, vw, ow)


def solution(mesh):
    return jax.shard_map(
        per_device,
        mesh=mesh,
        in_specs=(
            P("ctx", "head"),
            P(),
            P(),
            P("ctx", "head"),
            P("ctx", "head"),
            P("ctx", "head"),
            P("head", "ctx"),
        ),
        out_specs=P("ctx", "head"),
        check_vma=False,
    )
```

time: 400 us -> 116 us (0.29)
  waiting for transfers between devices: 275 us -> 16.6 us
  Pallas kernels: 0 us -> 80.2 us
  local copies, waits for them, and re-layouts: 46.1 us -> 3.48 us
  matrix products: 28.7 us -> 0.77 us
  between operations: 13.8 us -> 0.12 us
  starting transfers between devices: 23.5 us -> 12.5 us
  other arithmetic: 9.56 us -> 1.78 us
    all_gather x5 -> x0, waiting for transfers between devices: 249 us -> none  [the longest x1 79.5 us: per_device(): lax.all_gather(v_weight, 'ctx', axis=0, tiled=True)]
    pallas_call x0 -> x1, Pallas kernels: none -> 80.2 us  [fused(): pl.pallas_call(body, out_shape=jax.ShapeDtypeStruct((128, 1024), BF16), i...]
    unnamed x16, local copies, waits for them, and re-layouts: 31.2 us -> 1.9 us
    dot_general x68 -> x3, matrix products: 28.7 us -> 0.77 us  [the longest x1 0.29 us: relayout(): jnp.dot(here.astype(BF16), upper, preferred_element_type=F32)]
    reduce_scatter x1 -> x0, waiting for transfers between devices: 20.2 us -> none  [per_device(): lax.psum_scatter(partial_out, 'head', scatter_dimension=1, tiled=True)]
    all_to_all x1, waiting for transfers between devices: 0.01 us -> 16.6 us  [relayout(): lax.all_to_all(outgoing.reshape(devices, cap, width), 'ctx', split_axis=0...]
    ppermute x3 -> x0, starting transfers between devices: 11 us -> none  [shifted(): return lax.ppermute(x, axis, pairs)]
    another operation x7 -> x1, other arithmetic: 5.15 us -> 0.01 us  [relayout(): jnp.stack([jnp.sum(jnp.where(here & (order == j), table % rows_dev + 1, 0...]
  transfers between devices with their start and end apart: 10 -> 1, of which waited for: 9 -> 1; matrix products, arithmetic and copies ran while one was open for 19% -> 1% of each run, Pallas kernels for 0% -> 0%
where the time goes in v1:
time: 116 us; the launch traced here: 115 us
  Pallas kernels  80.2 us (69%)
  waiting for transfers between devices  16.6 us (14%)
  starting transfers between devices  12.5 us (11%)
  local copies, waits for them, and re-layouts  3.48 us (3%)
  other arithmetic  1.78 us (2%)
    pallas_call x1, Pallas kernels, fused(): pl.pallas_call(body, out_shape=jax.ShapeDtypeStruct((128, 1024), BF16), i...  80.2 us
    all_to_all x1, waiting for transfers between devices, relayout(): lax.all_to_all(outgoing.reshape(devices, cap, width), 'ctx', split_axis=0...  16.6 us
    all_to_all x1, starting transfers between devices, relayout(): lax.all_to_all(outgoing.reshape(devices, cap, width), 'ctx', split_axis=0...  12.5 us
  transfers between devices with their start and end apart: 1, of which 1 were waited for; matrix products, arithmetic and copies ran while one was open for 1% of the time, Pallas kernels for 0%

profile of v1, /device:TPU:5, one launch (start us, length us, event | category | flops | bytes accessed | tf_op | source)
XLA Modules:
  0.0 115.5 jit_solution(3850848140978072834)
XLA Ops:
  0.0 0.0 copy-start
  0.0 0.8 and_select_fusion
  0.8 0.2 convert_reduce_fusion
  1.0 0.8 multiply_add_fusion
  1.8 0.0 copy-done
  1.8 0.3 convolution_convert_fusion
  2.0 1.0 reshape.44
  3.1 0.0 copy-start.6
  3.1 12.5 %all-to-all-start = ((bf16[64,3,1024]{2,1,0:T(4,128)(2,1)}), bf16[64,3,1024]{2,1,0:T(4,128)(2,1)S(1)}, u32[]{:S(2)}, u32[]{:S(2)}) async-start(bf16[64,3,1024]{2,1,0:T(4,128)(2,1)} %reshape.44), calls=%async_computation | async-start | bytes 1048576 | tf_op jit(solution)/shard_map/all_to_all | solution.py:531
  15.5 0.0 copy-done.6
  15.5 0.0 copy-start.5
  15.5 0.3 select_reduce_fusion.2
  15.9 0.1 copy.11
  16.0 0.1 eq.71
  16.1 0.3 copy-done.5
  16.4 0.2 copy.12.refs_5_
  16.6 16.6 %all-to-all-done = bf16[64,3,1024]{2,1,0:T(4,128)(2,1)S(1)} async-done(((bf16[64,3,1024]{2,1,0:T(4,128)(2,1)}), bf16[64,3,1024]{2,1,0:T(4,128)(2,1)S(1)}, u32[]{:S(2)}, u32[]{:S(2)}) %all-to-all-start) | async-done | bytes 393248 | tf_op jit(solution)/shard_map/all_to_all | solution.py:531
  33.2 0.3 reshape.45
  33.6 0.0 copy-start.1
  33.6 0.0 copy-start.2
  33.6 0.0 copy-start.3
  33.6 0.2 convolution_convert_fusion.1.refs_0_
  33.8 0.0 copy-start.4
  33.9 0.6 copy-done.1
  34.5 0.0 copy-done.2
  34.5 0.0 copy-done.3
  34.5 0.0 copy-done.4
  34.5 80.2 %shard_map.73 = bf16[128,1024]{1,0:T(8,128)(2,1)S(1)} custom-call(bf16[128,1024]{1,0:T(8,128)(2,1)S(1)} %convolution_convert_fusion.1.refs_0_, s32[1,64]{1,0:T(1,128)S(1)} %bitcast.50, bf16[64,1024]{1,0:T(8,128)(2,1)S(1)} %copy-done.1, bf16[64,128]{1,0:T(8,128)(2,1)S(1)} %copy-done.2, bf16[64,128]{1,0:T(8,128)(2,1)S(1)} %copy-done.3, ...), custom_call_target="tpu_custom_call" | custom-call | tf_op jit(solution)/shard_map/pallas_call | solution.py:508
  114.8 0.7 copy.14
  (3 shorter events, 0.0 us)
Async XLA Ops:
  0.0 1.8 %copy-start = (bf16[128,1024]{1,0:T(8,128)(2,1)S(1)}, bf16[128,1024]{1,0:T(8,128)(2,1)}, u32[]{:S(2)}) copy-start(bf16[128,1024]{1,0:T(8,128)(2,1)} %param.7) | copy-start | bytes 786436
  3.1 12.5 %copy-start.6 = (s32[8192]{0:T(1024)S(1)}, s32[8192]{0:T(1024)}, u32[]{:S(2)}) copy-start(s32[8192]{0:T(1024)} %param.8) | copy-start | bytes 98308
  3.1 30.2 %all-to-all-start = ((bf16[64,3,1024]{2,1,0:T(4,128)(2,1)}), bf16[64,3,1024]{2,1,0:T(4,128)(2,1)S(1)}, u32[]{:S(2)}, u32[]{:S(2)}) async-start(bf16[64,3,1024]{2,1,0:T(4,128)(2,1)} %reshape.44), calls=%async_computation | async-start | bytes 1048576 | tf_op jit(solution)/shard_map/all_to_all | solution.py:531
  15.5 0.9 copy-start.5
  33.6 0.9 copy-start.1
  33.6 0.9 copy-start.2
  33.6 0.9 copy-start.3
  33.8 0.7 copy-start.4

commit v2 on v1

v2 whole, which is shorter than its diff:
```python
import math

import jax
import jax.numpy as jnp
from jax import lax
from jax.experimental import pallas as pl
from jax.experimental.pallas import tpu as pltpu
from jax.sharding import PartitionSpec as P

MESH = pl.DeviceIdType.MESH
F32 = jnp.float32
BF16 = jnp.bfloat16
ROPE_BASE = 500000.0
HD = 128

DZ = (0, 1, -1, 2, -2, 3, -3, 4)
DY = (0, 1, -1, 2)
ZS = {d: i for i, d in enumerate(DZ)}
YS = {d: i for i, d in enumerate(DY)}
GROUPS = ((0, 1), (1, 3), (3, 5), (5, 7), (7, 8))
WIDE_GROUPS = ((0, 3), (3, 7), (7, 8))

LINK_RATE, LINK_LATENCY = 47.0, 2.4
PEER_RATE, PEER_LATENCY = 400.0, 1.0
AHEAD = 1.0


class Node:
    def __init__(self, name, link, deps, size, prio=(0,), src=None, dst=None):
        self.name, self.link, self.deps, self.size, self.prio = name, link, deps, size, prio
        self.src, self.dst = src, dst


def gather_messages(tag, rows, width1, width2, ready, rank, groups=GROUPS):
    out = []
    half = rows // 2
    size1 = rows * width1 * 2e-3
    size2 = rows * width2 * 2e-3
    full, top, bottom = (0, rows), (0, half), (half, half)

    def one(dz, dy, part):
        return (tag + "1", ZS[dz], YS[dy], part)

    def pair(dz, which):
        return (tag + "1", ZS[dz], (2 * which, 2), full)

    def two(dy, dz, part):
        return (tag + "2", YS[dy], ZS[dz], part)

    def group(dy, g):
        lo, hi = groups[g]
        return (tag + "2", YS[dy], (lo, hi - lo), full)

    def add(name, link, src, dst, deps, size, prio):
        out.append(Node(tag + name, link, [tag + d for d in deps] + ready, size, (rank,) + prio, src, dst))

    if width1:
        add("1y+1", "+y", one(0, 0, full), one(0, -1, full), [], size1, (0, 1))
        add("1y-1", "-y", one(0, 0, full), one(0, 1, full), [], size1, (0, 1))
        add("1y+2", "+y", one(0, -1, top), one(0, 2, top), ["1y+1"], size1 / 2, (0, 2))
        add("1y-2", "-y", one(0, 1, bottom), one(0, 2, bottom), ["1y-1"], size1 / 2, (0, 2))
    first = {0: ["1y-1"], 1: ["1y+1", "1y+2", "1y-2"]}
    for which in (0, 1) if width1 else ():
        for sign, link in ((1, "+z"), (-1, "-z")):
            mark = "+" if sign > 0 else "-"
            for step in (1, 2, 3, 4):
                if step == 4 and (sign > 0) != (which == 0):
                    continue
                deps = first[which] if step == 1 else [f"1z{which}{mark}{step - 1}"]
                far = 4 if step == 4 else -sign * step
                add(f"1z{which}{mark}{step}", link, pair(-sign * (step - 1), which), pair(far, which), deps,
                    2 * size1, (1, step))
    for sign, link in ((1, "+z"), (-1, "-z")):
        mark = "+" if sign > 0 else "-"
        for step in (1, 2, 3, 4):
            deps = [] if step == 1 else [f"2z{mark}{step - 1}"]
            part = full if step < 4 else (top if sign > 0 else bottom)
            far = 4 if step == 4 else -sign * step
            add(f"2z{mark}{step}", link, two(0, -sign * (step - 1), part), two(0, far, part), deps,
                size2 if step < 4 else size2 / 2, (0, step))
    for g, (lo, hi) in enumerate(groups):
        deps = []
        for dz in DZ[lo:hi]:
            deps += z_messages(dz)
        amount = size2 * (hi - lo)
        add(f"2y{g}+1", "+y", group(0, g), group(-1, g), deps, amount, (1, g))
        add(f"2y{g}-1", "-y", group(0, g), group(1, g), deps, amount, (1, g))
        if g % 2 == 0:
            add(f"2y{g}+2", "+y", group(-1, g), group(2, g), [f"2y{g}+1"], amount, (1, g))
        else:
            add(f"2y{g}-2", "-y", group(1, g), group(2, g), [f"2y{g}-1"], amount, (1, g))
    return out


def z_messages(dz):
    if dz == 0:
        return []
    return ["2z+4", "2z-4"] if dz == 4 else [f"2z{'+' if dz < 0 else '-'}{abs(dz)}"]


def needs(tag, dz, which, groups=GROUPS):
    g = [i for i, (lo, hi) in enumerate(groups) if lo <= ZS[dz] < hi][0]
    if which == 0:
        names = z_messages(dz) + [f"2y{g}-1"]
    else:
        names = [f"2y{g}+1", f"2y{g}+2" if g % 2 == 0 else f"2y{g}-2"]
    if tag != "k":
        if dz == 0:
            names += ["1y-1"] if which == 0 else ["1y+1", "1y+2", "1y-2"]
        elif dz == 4:
            names += ["1z0+4"] if which == 0 else ["1z1-4"]
        else:
            names += [f"1z{which}{'+' if dz < 0 else '-'}{abs(dz)}"]
    return [tag + n for n in names]


def all_nodes():
    x_all = ["x+a", "x+b", "x-a", "x-b", "xs+", "xs-", "xs2"]
    nodes = [
        Node("w1", "peer", [], 33),
        Node("w2", "peer", [], 33),
        Node("w3", "peer", [], 17),
        Node("r+z", "+z", [], 384, (-2,)),
        Node("r-z", "-z", [], 384, (-2,)),
        Node("r+y", "+y", [], 192, (-2,)),
        Node("r-y", "-y", [], 192, (-2,)),
        Node("rows", "peer", ["r+z", "r-z", "r+y", "r-y"], 384, (-1,)),
        Node("x+a", "+x", ["place"], 131, (0, 0)),
        Node("x+b", "+x", ["place"], 131, (0, 1)),
        Node("x-b", "-x", ["place"], 131, (0, 0)),
        Node("x-a", "-x", ["place"], 131, (0, 1)),
        Node("x+2", "+x", ["x+a"], 131, (0, 2)),
        Node("x-2", "-x", ["x-b"], 131, (0, 2)),
        Node("xs+", "peer", ["x+a", "x+b"], 262, (1,)),
        Node("xs-", "peer", ["x-a", "x-b"], 262, (1,)),
        Node("xs2", "peer", ["x+2", "x-2"], 262, (1,)),
        Node("h0", "peer", ["kv"], 65, (0,)),
        Node("h1", "+y", ["kv"], 85, (-1, 0)),
        Node("h2", "+y", ["kv"], 65, (-1, 1)),
        Node("h1s", "peer", ["h1"], 65, (0,)),
        Node("h2s", "peer", ["h2"], 33, (0,)),
    ]
    nodes += gather_messages("k", 128, 0, 128, ["w3"], 0, WIDE_GROUPS)
    nodes += gather_messages("q", 128, 256, 256, ["w1", "w2"], 1)
    nodes += gather_messages("o", 64, 384, 640, [], 2)

    def step(name, deps, span):
        nodes.append(Node(name, "core", deps, span, (len(nodes),)))

    step("tables", [], 1.5)
    step("place", ["rows"], 1.3)
    every = [n for dz in DZ for which in (0, 1) for n in needs("k", dz, which, WIDE_GROUPS)]
    step("kv", every + x_all + ["tables"], 1.0)
    for dz in DZ:
        step(f"Q{dz}", needs("q", dz, 0) + needs("q", dz, 1) + x_all, 0.45)
    step("rope", [f"Q{dz}" for dz in DZ] + ["tables"], 0.6)
    step("vt", ["h0", "h1", "h2", "h1s", "h2s"], 0.2)
    for qb in (0, 1):
        for pair in (0, 1):
            step(f"A{qb}{pair}", ["rope", "vt"], 0.8)
            nodes.append(Node(f"a{qb}{pair}", "peer", [f"A{qb}{pair}"], 65))
    for dz in DZ:
        for which in (0, 1):
            step(f"O{dz},{which}", needs("o", dz, which) + [f"a{qb}{pair}" for qb in (0, 1) for pair in (0, 1)], 0.3)
    return nodes


def plan():
    nodes = all_nodes()
    free, arrival, actions = {}, {}, []
    pending = list(nodes)
    while pending:
        best = None
        by_link = {}
        for m in pending:
            if all(d in arrival for d in m.deps):
                at = max([arrival[d] for d in m.deps], default=0.0)
                by_link.setdefault(m.link, []).append((at, m))
        for link, options in by_link.items():
            begin = max(free.get(link, 0.0), min(at for at, _ in options))
            at, m = min(((at, m) for at, m in options if at <= begin), key=lambda p: p[1].prio)
            if best is None or begin < best[0]:
                best = (begin, m, at)
        begin, m, at = best
        if m.link == "core":
            span, latency = m.size, 0.0
        elif m.link == "peer":
            span, latency = m.size / PEER_RATE, PEER_LATENCY
        else:
            span, latency = m.size / LINK_RATE, LINK_LATENCY
        free[m.link] = begin + span
        arrival[m.name] = begin + span + latency
        pending.remove(m)
        if m.link == "core":
            actions.append((begin, 2, "step", m.name))
        else:
            actions.append((max(at, begin - AHEAD), 1, "send", m.name))
            actions.append((arrival[m.name], 0, "recv", m.name))
    actions.sort(key=lambda a: a[:2])
    return nodes, actions, arrival


def kernel(messages, actions, tokens, table, lens, qw, kw, vw, ow, out,
           k2, q1, q2, o1, o2, tk, tb, ln, wide, rows_out, rows_in, xs, acck, acc1, acc2, cs, bias, qs, kv, vt, att, part, rs,
           lsem, send, recv, rsend, rrecv, psend, precv):
    ctx, x = lax.axis_index("ctx"), lax.axis_index("head")
    z, y, core = ctx // 8, (ctx // 2) % 4, ctx % 2
    chip = ctx // 2
    other = 1 - core
    buffers = {"k2": k2, "q1": q1, "q2": q2, "o1": o1, "o2": o2}
    number = {m.name: i for i, m in enumerate(messages)}

    def at(dz, dy, which, dx=0):
        return ((lax.rem(z + dz + 8, 8) * 4 + lax.rem(y + dy + 4, 4)) * 2 + which, lax.rem(x + dx + 4, 4))

    def chip_at(by, which):
        return (lax.rem(chip + by + 32, 32) * 2 + which, x)

    across = at(0, 0, other)
    mine = pl.ds(pl.multiple_of(core * 64, 64), 64)
    theirs = pl.ds(pl.multiple_of(other * 64, 64), 64)

    def columns(which, part):
        lo, n = ((0, 256), (256, 256))[part]
        return pl.ds(pl.multiple_of(which * 512 + lo, 128), n)

    def local(i, src, dst):
        return pltpu.make_async_copy(src, dst, lsem.at[i])

    own_kv = [local(7, kw, k2.at[0, 0, mine]), local(7, vw, k2.at[0, 0, mine])]
    early = [local(0, tokens, tk), local(1, table, tb), local(2, lens, ln)]
    late = [
        local(3, qw.at[:, columns(core, 0)], q1.at[0, 0, mine]),
        local(4, qw.at[:, columns(core, 1)], q2.at[0, 0, mine]),
        local(5, ow.at[:, pl.ds(0, 384)], o1.at[0, 0]),
        local(6, ow.at[:, pl.ds(384, 640)], o2.at[0, 0]),
    ]
    for copy in early + late:
        copy.start()
    for which in (0, 1):

        @pl.when(core == which)
        def _():
            own_kv[which].start()

    peers = [across] + [at(0, 0, which, dx) for dx in (1, 2, 3) for which in (0, 1)]
    peers += [chip_at(by, other) for by in (1, 2, -1, -2)]
    barrier = pltpu.get_barrier_semaphore()
    for peer in peers:
        pl.semaphore_signal(barrier, inc=1, device_id=peer, device_id_type=MESH)

    @pl.loop(1, 32)
    def _(by):
        pl.semaphore_signal(barrier, inc=1, device_id=chip_at(by, core), device_id_type=MESH)

    for copy in early:
        copy.wait()
    i0 = lax.broadcasted_iota(jnp.int32, (128, 128), 0)
    i1 = lax.broadcasted_iota(jnp.int32, (128, 128), 1)
    goal_row = jnp.broadcast_to((tb[pl.ds(ctx, 1), :] >> 7).astype(F32), (128, 128))
    goal_col = jnp.sum(jnp.where(i0 == i1, goal_row, 0.0), axis=1, keepdims=True)
    rank = jnp.sum(jnp.where((goal_col == goal_row) & (i0 < i1), 1.0, 0.0), axis=0, keepdims=True)
    slot = 3.0 * goal_row[:1] + rank
    pick = jnp.where(lax.broadcasted_iota(jnp.int32, (192, 128), 0).astype(F32) == slot, 1.0, 0.0).astype(BF16)
    picked = jnp.dot(pick, tk[...], preferred_element_type=F32)
    for j in range(8):
        wide[pl.ds(j, 192, stride=8), :] = picked[:, 128 * j : 128 * j + 128]
    rows_out[...] = wide[0:1536, :].astype(BF16).reshape(32, 48, 128)
    pl.semaphore_wait(barrier, len(peers) + 31)

    def row_copy(by, coming=False):
        goal, origin = lax.rem(chip + by, 32), lax.rem(chip + 32 - by, 32)
        src, dst = rows_out.at[goal], rows_in.at[chip, core]
        if coming:
            src = dst = rows_in.at[origin, core]
        return pltpu.make_async_remote_copy(
            src_ref=src, dst_ref=dst, send_sem=rsend.at[by], recv_sem=rrecv.at[by],
            device_id=chip_at(by, core), device_id_type=MESH,
        )

    @pl.loop(0, 31)
    def _(i):
        row_copy(1 + lax.rem(i + 15, 31)).start()

    keep = local(8, rows_out.at[chip], rows_in.at[chip, core])
    keep.start()
    for copy in late:
        copy.wait()
    own_kv[0].wait()

    x_low, x_high, x_far = lax.rem(x + 3, 4), lax.rem(x + 1, 4), lax.rem(x + 2, 4)
    top, bottom = pl.ds(0, 64), pl.ds(64, 64)
    far_keys, near_keys, own_keys, upper_keys = pl.ds(0, 128), pl.ds(128, 256), pl.ds(384, 256), pl.ds(512, 128)
    special = {
        "w1": (qw.at[:, columns(other, 0)], q1.at[0, 0, mine], q1.at[0, 0, theirs], across),
        "w2": (qw.at[:, columns(other, 1)], q2.at[0, 0, mine], q2.at[0, 0, theirs], across),
        "rows": (rows_in.at[:, core], rows_in.at[:, core], rows_in.at[:, other], across),
        "x+a": (xs.at[x, core, top], xs.at[x, core, top], xs.at[x_low, core, top], at(0, 0, core, 1)),
        "x+b": (xs.at[x, core, bottom], xs.at[x, core, bottom], xs.at[x_low, core, bottom], at(0, 0, core, 1)),
        "x-a": (xs.at[x, core, top], xs.at[x, core, top], xs.at[x_high, core, top], at(0, 0, core, -1)),
        "x-b": (xs.at[x, core, bottom], xs.at[x, core, bottom], xs.at[x_high, core, bottom], at(0, 0, core, -1)),
        "x+2": (xs.at[x_low, core, top], xs.at[x_low, core, top], xs.at[x_far, core, top], at(0, 0, core, 1)),
        "x-2": (xs.at[x_high, core, bottom], xs.at[x_high, core, bottom], xs.at[x_far, core, bottom],
                at(0, 0, core, -1)),
        "xs+": (xs.at[x_low, core], xs.at[x_low, core], xs.at[x_low, other], across),
        "xs-": (xs.at[x_high, core], xs.at[x_high, core], xs.at[x_high, other], across),
        "xs2": (xs.at[x_far, core], xs.at[x_far, core], xs.at[x_far, other], across),
        "h0": (kv.at[core, own_keys], kv.at[core, own_keys], kv.at[other, own_keys], across),
        "h1": (kv.at[core, own_keys], kv.at[core, near_keys], kv.at[core, near_keys], chip_at(1, core)),
        "h2": (kv.at[core, upper_keys], kv.at[core, far_keys], kv.at[core, far_keys], chip_at(2, core)),
        "h1s": (kv.at[core, near_keys], kv.at[core, near_keys], kv.at[other, near_keys], across),
        "h2s": (kv.at[core, far_keys], kv.at[core, far_keys], kv.at[other, far_keys], across),
    }
    for qb in (0, 1):
        for pair in (0, 1):
            special[f"a{qb}{pair}"] = (att.at[core, pair, qb], att.at[core, pair, qb], att.at[other, pair, qb], across)
    to = {"+z": at(1, 0, core), "-z": at(-1, 0, core), "+y": at(0, 1, core), "-y": at(0, -1, core)}

    def view(place):
        name, a, b, (lo, n) = place
        b = pl.ds(*b) if isinstance(b, tuple) else b
        return buffers[name].at[a, b, pl.ds(lo, n)]

    def remote(src, dst, ssem, rsem, device):
        return pltpu.make_async_remote_copy(
            src_ref=src, dst_ref=dst, send_sem=ssem, recv_sem=rsem, device_id=device, device_id_type=MESH
        )

    def copy_of(m, coming=False):
        i = number[m.name]
        if m.name in special:
            src, dst, land, device = special[m.name]
        else:
            src, dst, land, device = view(m.src), view(m.dst), view(m.dst), to[m.link]
        if coming:
            src = dst = land
        return remote(src, dst, send.at[i], recv.at[i], device)

    by_name = {m.name: m for m in messages}

    def kv_copy(which):
        i = number["w3"]
        src = (vw, kw)[which]
        return remote(src, k2.at[0, 0, mine], send.at[i], recv.at[i], across)

    def place():
        t = tb[...]
        upper = jnp.where(i0 < i1, 1.0, 0.0).astype(BF16)
        landing = []
        for half in (0, 1):
            here = (t >> 7) == 2 * chip + half
            nth = jnp.dot(jnp.where(here, 1.0, 0.0).astype(BF16), upper, preferred_element_type=F32)
            row = ((t & 255) + 1).astype(F32)
            for k in range(3):
                landing.append(jnp.sum(jnp.where(here & (nth == float(k)), row, 0.0), axis=1, keepdims=True))
        goal = jnp.concatenate(landing, axis=0)
        lane = lax.broadcasted_iota(jnp.int32, (384, 256), 1).astype(F32) + 1.0
        spot = jnp.transpose(jnp.where(goal == lane, 1.0, 0.0)).astype(BF16)
        wide[...] = rows_in[...].astype(F32).reshape(3072, 128)
        for j in range(8):
            rows = [wide[pl.ds(8 * n + j, 64, stride=48), :] for n in range(6)]
            rows = jnp.concatenate(rows, axis=0).astype(BF16)
            found = jnp.dot(spot, rows, preferred_element_type=F32).astype(BF16)
            xs[x, :, :, 128 * j : 128 * j + 128] = found.reshape(2, 128, 128)

    pseudo = ("r+z", "r-z", "r+y", "r-y")

    def start_message(name):
        if name == "rows":
            keep.wait()

            @pl.loop(1, 32)
            def _(by):
                row_copy(by, True).wait_recv()

        if name == "w3":
            for which in (0, 1):

                @pl.when(core == which)
                def _():
                    kv_copy(which).start()

        elif name not in pseudo:
            copy_of(by_name[name]).start()

    def finish_message(name):
        if name == "w3":
            i = number["w3"]
            land = k2.at[0, 0, theirs]
            remote(land, land, send.at[i], recv.at[i], across).wait_recv()
        elif name not in pseudo:
            copy_of(by_name[name], True).wait_recv()

    def tables():
        base = chip * 256
        d0 = lax.broadcasted_iota(jnp.int32, (64, 64), 0)
        d1 = lax.broadcasted_iota(jnp.int32, (64, 64), 1)
        spread = jnp.broadcast_to(ln[...].astype(F32), (64, 64))
        end_col = jnp.sum(jnp.where(d1 <= d0, spread, 0.0), axis=1, keepdims=True)
        len_col = jnp.sum(jnp.where(d1 == d0, spread, 0.0), axis=1, keepdims=True)
        end_row = jnp.sum(jnp.where(d0 <= d1, jnp.broadcast_to(len_col, (64, 64)), 0.0), axis=0, keepdims=True)
        row_id = (base + lax.broadcasted_iota(jnp.int32, (64, 256), 1)).astype(F32)
        before = row_id >= end_col
        q_doc = jnp.sum(jnp.where(before, 1.0, 0.0), axis=0, keepdims=True)
        position = row_id - jnp.sum(jnp.where(before, len_col, 0.0), axis=0, keepdims=True)
        turn = lax.broadcasted_iota(jnp.int32, (64, 256), 0).astype(F32)
        angle = position * jnp.exp(turn * (-2.0 / HD * math.log(ROPE_BASE)))
        cs[...] = jnp.transpose(jnp.concatenate([jnp.cos(angle), jnp.sin(angle)], axis=0))
        key_id = base - 384 + lax.broadcasted_iota(jnp.int32, (640, 64), 0)
        k_doc = jnp.sum(jnp.where(key_id.astype(F32) >= end_row, 1.0, 0.0), axis=1, keepdims=True)
        for qb in (0, 1):
            lo = 128 * qb
            kid = base - 384 + lo + lax.broadcasted_iota(jnp.int32, (512, 128), 0)
            qid = base + lo + lax.broadcasted_iota(jnp.int32, (512, 128), 1)
            allowed = (k_doc[lo : lo + 512] == q_doc[:, lo : lo + 128]) & (kid <= qid) & (kid >= 0)
            bias[qb] = jnp.where(allowed, 0.0, -jnp.inf)

    def columns_of(dz):
        zz = lax.rem(z + dz + 8, 8)
        parts = []
        for dy in DY:
            lane = pl.multiple_of((lax.rem(zz, 2) * 4 + lax.rem(y + dy + 4, 4)) * 128, 128)
            parts.append(xs[zz // 2, :, :, pl.ds(lane, 128)].reshape(256, 128))
        return jnp.concatenate(parts, axis=1)

    def project(dz):
        s = ZS[dz]
        lhs = columns_of(dz)
        one = jnp.dot(lhs, q1[s].reshape(512, 256), preferred_element_type=F32)
        two = jnp.dot(lhs, q2[:, s].reshape(512, 256), preferred_element_type=F32)
        if dz == 0:
            acc1[...] = one
            acc2[...] = two
        else:
            acc1[...] += one
            acc2[...] += two

    def turned_pairs():
        table = cs[...]
        swapped = pltpu.roll(table, 64, 1)
        low = lax.broadcasted_iota(jnp.int32, (256, 128), 1) < 64
        return jnp.where(low, table, swapped), jnp.where(low, -swapped, table)

    def rope(e):
        cosine, sine = turned_pairs()
        return e * cosine + pltpu.roll(e, 64, 1) * sine

    def make_kv():
        raw = None
        for dz in DZ:
            term = jnp.dot(columns_of(dz), k2[:, ZS[dz]].reshape(512, 128), preferred_element_type=F32)
            raw = term if raw is None else raw + term
        acck[...] = raw
        raw = acck[...]
        kv[core, 384:640] = jnp.where(core == 0, rope(raw), raw).astype(BF16)

    def rope_queries():
        for h in range(4):
            e = acc1[:, 128 * h : 128 * h + 128] if h < 2 else acc2[:, 128 * (h - 2) : 128 * (h - 2) + 128]
            turned_e = rope(e).astype(BF16)
            for qb in (0, 1):
                qs[qb, h // 2, 128 * (h % 2) : 128 * (h % 2) + 128] = turned_e[128 * qb : 128 * qb + 128]

    def turn_values():
        eye = (
            lax.broadcasted_iota(jnp.int32, (128, 128), 0) == lax.broadcasted_iota(jnp.int32, (128, 128), 1)
        ).astype(F32).astype(BF16)
        vt[...] = lax.dot_general(eye, kv[1], (((1,), (1,)), ((), ())), preferred_element_type=F32).astype(BF16)

    def attend(qb, pair):
        keys = kv[0, 128 * qb : 128 * qb + 512]
        scores = lax.dot_general(keys, qs[qb, pair], (((1,), (1,)), ((), ())), preferred_element_type=F32)
        mask = bias[qb]
        scores = scores * (1.0 / math.sqrt(HD)) + jnp.concatenate([mask, mask], axis=1)
        expo = jnp.exp(scores - jnp.max(scores, axis=0, keepdims=True))
        denominator = jnp.sum(expo, axis=0, keepdims=True)
        summed = jnp.dot(vt[:, 128 * qb : 128 * qb + 512], expo.astype(BF16), preferred_element_type=F32)
        result = (summed / denominator).astype(BF16)
        for h in (0, 1):
            att[core, pair, qb, 128 * h : 128 * h + 128] = result[:, 128 * h : 128 * h + 128]

    def part_copy(dz, which, t, start):
        s = ZS[dz]
        zz = lax.rem(z + dz + 8, 8)
        goal = zz // 2
        here = (goal == x) & (core == t)
        sem = precv.at[core, x, lax.rem(zz, 2), which]
        land = rs.at[core, x, lax.rem(zz, 2), which]

        @pl.when(jnp.logical_not(here))
        def _():
            copy = remote(part.at[s, which, t], land, psend.at[s, which, t], sem, (chip * 2 + t, goal))
            copy.start() if start else copy.wait_send()

        if start:

            @pl.when(here)
            def _():
                pltpu.make_async_copy(part.at[s, which, t], land, sem).start()

    def out_project(dz, which):
        s = ZS[dz]
        dy = slice(2 * which, 2 * which + 2)
        weights = jnp.concatenate([att[:, :, 0].reshape(1024, 128), att[:, :, 1].reshape(1024, 128)], axis=1)
        total = jnp.dot(o1[s, dy].reshape(128, 384), weights[:384], preferred_element_type=F32)
        total += jnp.dot(o2[dy, s].reshape(128, 640), weights[384:], preferred_element_type=F32)
        total = total.astype(BF16)
        for t in (0, 1):
            part[s, which, t] = total[:, 128 * t : 128 * t + 128]
            part_copy(dz, which, t, True)

    def run(name):
        if name == "tables":
            tables()
        elif name == "place":
            place()
        elif name == "kv":
            make_kv()
        elif name == "rope":
            rope_queries()
        elif name == "vt":
            turn_values()
        elif name[0] == "A":
            attend(int(name[1]), int(name[2]))
        elif name[0] == "Q":
            project(int(name[1:]))
        else:
            dz, which = name[1:].split(",")
            out_project(int(dz), int(which))

    for _, _, kind, name in actions:
        if kind == "send":
            start_message(name)
        elif kind == "recv":
            finish_message(name)
        else:
            run(name)

    @pl.loop(1, 32)
    def _(by):
        row_copy(by).wait_send()

    kv_copy(0).wait_send()
    for m in messages:
        if m.name not in pseudo and m.name != "w3":
            copy_of(m).wait_send()
    for dz in DZ:
        for which in (0, 1):
            for t in (0, 1):
                part_copy(dz, which, t, False)
    for zz in (0, 1):
        sums = []
        for c in (0, 1):
            total = None
            for g in range(4):
                for which in (0, 1):
                    land = rs.at[c, g, zz, which]
                    remote(land, land, psend.at[0, 0, 0], precv.at[c, g, zz, which], across).wait_recv()
                term = rs[c, g, zz].reshape(256, 128).astype(F32)
                total = term if total is None else total + term
            sums.append(total)
        for dy in DY:
            s = YS[dy]
            block = jnp.concatenate([sums[0][64 * s : 64 * s + 64], sums[1][64 * s : 64 * s + 64]], axis=0)
            lane = pl.multiple_of((zz * 4 + lax.rem(y + dy + 4, 4)) * 128, 128)
            out[:, pl.ds(lane, 128)] = jnp.transpose(block).astype(BF16)


def per_device(tokens, context_row, lengths, qw, kw, vw, ow):
    nodes, actions, _ = plan()
    messages = [n for n in nodes if n.link != "core"]
    count = len(messages)
    dma = pltpu.SemaphoreType.DMA
    scratch = [
        pltpu.VMEM((4, 8, 128, 128), BF16),
        pltpu.VMEM((8, 4, 128, 256), BF16),
        pltpu.VMEM((4, 8, 128, 256), BF16),
        pltpu.VMEM((8, 4, 64, 384), BF16),
        pltpu.VMEM((4, 8, 64, 640), BF16),
        pltpu.VMEM((128, 1024), BF16),
        pltpu.VMEM((64, 128), jnp.int32),
        pltpu.VMEM((1, 64), jnp.int32),
        pltpu.VMEM((3072, 128), F32),
        pltpu.VMEM((32, 48, 128), BF16),
        pltpu.VMEM((32, 2, 48, 128), BF16),
        pltpu.VMEM((4, 2, 128, 1024), BF16),
        pltpu.VMEM((256, 128), F32),
        pltpu.VMEM((256, 256), F32),
        pltpu.VMEM((256, 256), F32),
        pltpu.VMEM((256, 128), F32),
        pltpu.VMEM((2, 512, 128), F32),
        pltpu.VMEM((2, 2, 256, 128), BF16),
        pltpu.VMEM((2, 640, 128), BF16),
        pltpu.VMEM((128, 640), BF16),
        pltpu.VMEM((2, 2, 2, 256, 128), BF16),
        pltpu.VMEM((8, 2, 2, 128, 128), BF16),
        pltpu.VMEM((2, 4, 2, 2, 128, 128), BF16),
        dma((9,)),
        dma((count,)),
        dma((count,)),
        dma((32,)),
        dma((32,)),
        dma((8, 2, 2)),
        dma((2, 4, 2, 2)),
    ]

    def body(*refs):
        kernel(messages, actions, *refs)

    return pl.pallas_call(
        body,
        out_shape=jax.ShapeDtypeStruct((128, 1024), BF16),
        in_specs=[pl.BlockSpec(memory_space=pltpu.HBM)] * 7,
        out_specs=pl.BlockSpec(memory_space=pltpu.VMEM),
        scratch_shapes=scratch,
        compiler_params=pltpu.CompilerParams(
            collective_id=0, has_side_effects=True, vmem_limit_bytes=63 * 2**20
        ),
    )(tokens, context_row.reshape(64, 128), lengths.reshape(1, 64), qw, kw, vw, ow.T)


def solution(mesh):
    return jax.shard_map(
        per_device,
        mesh=mesh,
        in_specs=(
            P("ctx", "head"),
            P(),
            P(),
            P("ctx", "head"),
            P("ctx", "head"),
            P("ctx", "head"),
            P("head", "ctx"),
        ),
        out_specs=P("ctx", "head"),
        check_vma=False,
    )
```

time: 116 us -> 92.3 us (0.80)
  waiting for transfers between devices: 16.6 us -> 0 us
  starting transfers between devices: 12.5 us -> 0 us
  Pallas kernels: 80.2 us -> 90.5 us
  local copies, waits for them, and re-layouts: 3.48 us -> 1.67 us
  other arithmetic: 1.78 us -> 0 us
    all_to_all x1 -> x0, waiting for transfers between devices: 16.6 us -> none  [relayout(): lax.all_to_all(outgoing.reshape(devices, cap, width), 'ctx', split_axis=0...]
    all_to_all x1 -> x0, starting transfers between devices: 12.5 us -> none  [relayout(): lax.all_to_all(outgoing.reshape(devices, cap, width), 'ctx', split_axis=0...]
    pallas_call x1, Pallas kernels: 80.2 us -> 90.5 us  [per_device(): pl.pallas_call(body, out_shape=jax.ShapeDtypeStruct((128, 1024), BF16), i...]
    reshape x2 -> x0, local copies, waits for them, and re-layouts: 1.35 us -> none  [the longest x1 1.02 us: relayout(): outgoing.reshape(devices, cap, width)]
  transfers between devices with their start and end apart: 1 -> 0, of which waited for: 1 -> 0; matrix products, arithmetic and copies ran while one was open for 1% -> 0% of each run, Pallas kernels for 0% -> 0%
where the time goes in v2:
time: 92.3 us; the launch traced here: 92.1 us
  Pallas kernels  90.5 us (98%)
  local copies, waits for them, and re-layouts  1.67 us (2%)
    pallas_call x1, Pallas kernels, per_device(): pl.pallas_call(body, out_shape=jax.ShapeDtypeStruct((128, 1024), BF16), i...  90.5 us

profile of v2, /device:TPU:5, one launch (start us, length us, event | category | flops | bytes accessed | tf_op | source)
XLA Modules:
  0.0 92.1 jit_solution(9148579557516534447)
XLA Ops:
  0.0 90.5 %shard_map.73 = bf16[128,1024]{1,0:T(8,128)(2,1)} custom-call(bf16[128,1024]{1,0:T(8,128)(2,1)} %refs_0_.1, s32[64,128]{1,0:T(8,128)} %bitcast.4, s32[1,64]{1,0:T(1,128)} %bitcast.5, bf16[64,1024]{1,0:T(8,128)(2,1)} %refs_3_.1, bf16[64,128]{1,0:T(8,128)(2,1)} %refs_4_.1, bf16[64,128]{1,0:T(8,128)(2,1)} %refs_5_.1, bf16[64,1024]{1,0:T(8,128)(2,1)} %bitcast.3), custom_call_target="tpu_custom_call" | custom-call | tf_op jit(solution)/shard_map/pallas_call | solution.py:610
  90.5 1.7 %copy.9 = bf16[128,1024]{1,0:T(8,128)(2,1)} copy(bf16[128,1024]{1,0:T(8,128)(2,1)} %shard_map.73) | data formatting | bytes 524288

commit v3 on v2

--- a/solution.py
+++ b/solution.py
@@ -20,9 +20,10 @@
 GROUPS = ((0, 1), (1, 3), (3, 5), (5, 7), (7, 8))
 WIDE_GROUPS = ((0, 3), (3, 7), (7, 8))
 
-LINK_RATE, LINK_LATENCY = 47.0, 2.4
+LINK_RATE, LINK_LATENCY = 44, 3.2
 PEER_RATE, PEER_LATENCY = 400.0, 1.0
 AHEAD = 1.0
+EXTRA = {"r": 4.0, "x": 1.0, "h": 1.0, "a": 0.5}
 
 
 class Node:
@@ -188,6 +189,7 @@
             span, latency = m.size / PEER_RATE, PEER_LATENCY
         else:
             span, latency = m.size / LINK_RATE, LINK_LATENCY
+        latency += EXTRA.get(m.name[0], 0.0) if m.link != "core" and m.name != "rows" else 0.0
         free[m.link] = begin + span
         arrival[m.name] = begin + span + latency
         pending.remove(m)

time: 92.3 us -> 86.1 us (0.933)
  Pallas kernels: 90.5 us -> 84.3 us
    pallas_call x1, Pallas kernels: 90.5 us -> 84.3 us  [per_device(): pl.pallas_call(body, out_shape=jax.ShapeDtypeStruct((128, 1024), BF16), i...]
where the time goes in v3:
time: 86.1 us; the launch traced here: 86 us
  Pallas kernels  84.3 us (98%)
  local copies, waits for them, and re-layouts  1.67 us (2%)
    pallas_call x1, Pallas kernels, per_device(): pl.pallas_call(body, out_shape=jax.ShapeDtypeStruct((128, 1024), BF16), i...  84.3 us

profile of v3, /device:TPU:5, one launch (start us, length us, event | category | flops | bytes accessed | tf_op | source)
XLA Modules:
  0.0 86.0 jit_solution(10845815491676986001)
XLA Ops:
  0.0 84.3 %shard_map.73 = bf16[128,1024]{1,0:T(8,128)(2,1)} custom-call(bf16[128,1024]{1,0:T(8,128)(2,1)} %refs_0_.1, s32[64,128]{1,0:T(8,128)} %bitcast.4, s32[1,64]{1,0:T(1,128)} %bitcast.5, bf16[64,1024]{1,0:T(8,128)(2,1)} %refs_3_.1, bf16[64,128]{1,0:T(8,128)(2,1)} %refs_4_.1, bf16[64,128]{1,0:T(8,128)(2,1)} %refs_5_.1, bf16[64,1024]{1,0:T(8,128)(2,1)} %bitcast.3), custom_call_target="tpu_custom_call" | custom-call | tf_op jit(solution)/shard_map/pallas_call | solution.py:612
  84.3 1.7 %copy.9 = bf16[128,1024]{1,0:T(8,128)(2,1)} copy(bf16[128,1024]{1,0:T(8,128)(2,1)} %shard_map.73) | data formatting | bytes 524288

commit v4 on v3

--- a/solution.py
+++ b/solution.py
@@ -22,8 +22,8 @@
 
 LINK_RATE, LINK_LATENCY = 44, 3.2
 PEER_RATE, PEER_LATENCY = 400.0, 1.0
-AHEAD = 1.0
-EXTRA = {"r": 4.0, "x": 1.0, "h": 1.0, "a": 0.5}
+AHEAD = 2.0
+EXTRA = {"r": 6.0, "x": 1.0, "h": 1.0, "a": 0.5}
 
 
 class Node:
@@ -611,7 +611,7 @@
 
     return pl.pallas_call(
         body,
-        out_shape=jax.ShapeDtypeStruct((128, 1024), BF16),
+        out_shape=pltpu.VMEM((128, 1024), BF16),
         in_specs=[pl.BlockSpec(memory_space=pltpu.HBM)] * 7,
         out_specs=pl.BlockSpec(memory_space=pltpu.VMEM),
         scratch_shapes=scratch,

time: 86.1 us -> 83.1 us (0.965)
  Pallas kernels: 84.3 us -> 82.2 us
  local copies, waits for them, and re-layouts: 1.67 us -> 0.71 us
    pallas_call x1, Pallas kernels: 84.3 us -> 82.2 us  [per_device(): pl.pallas_call(body, out_shape=pltpu.VMEM((128, 1024), BF16), in_specs=[p...]
    unnamed x1, local copies, waits for them, and re-layouts: 1.67 us -> 0.71 us
where the time goes in v4:
time: 83.1 us; the launch traced here: 83 us
  Pallas kernels  82.2 us (99%)
    pallas_call x1, Pallas kernels, per_device(): pl.pallas_call(body, out_shape=pltpu.VMEM((128, 1024), BF16), in_specs=[p...  82.2 us

profile of v4, /device:TPU:5, one launch (start us, length us, event | category | flops | bytes accessed | tf_op | source)
XLA Modules:
  0.0 83.0 jit_solution(17169740340817892123)
XLA Ops:
  0.0 82.2 %shard_map.73 = bf16[128,1024]{1,0:T(8,128)(2,1)S(1)} custom-call(bf16[128,1024]{1,0:T(8,128)(2,1)} %refs_0_.1, s32[64,128]{1,0:T(8,128)} %bitcast.4, s32[1,64]{1,0:T(1,128)} %bitcast.5, bf16[64,1024]{1,0:T(8,128)(2,1)} %refs_3_.1, bf16[64,128]{1,0:T(8,128)(2,1)} %refs_4_.1, bf16[64,128]{1,0:T(8,128)(2,1)} %refs_5_.1, bf16[64,1024]{1,0:T(8,128)(2,1)} %bitcast.3), custom_call_target="tpu_custom_call" | custom-call | tf_op jit(solution)/shard_map/pallas_call | solution.py:612
  82.3 0.7 copy.9

commit v5 on v4

--- a/solution.py
+++ b/solution.py
@@ -546,11 +546,8 @@
     for m in messages:
         if m.name not in pseudo and m.name != "w3":
             copy_of(m).wait_send()
-    for dz in DZ:
-        for which in (0, 1):
-            for t in (0, 1):
-                part_copy(dz, which, t, False)
-    for zz in (0, 1):
+    for late_half in (0, 1):
+        zz = lax.rem(z + 1 + late_half, 2)
         sums = []
         for c in (0, 1):
             total = None
@@ -566,6 +563,10 @@
             block = jnp.concatenate([sums[0][64 * s : 64 * s + 64], sums[1][64 * s : 64 * s + 64]], axis=0)
             lane = pl.multiple_of((zz * 4 + lax.rem(y + dy + 4, 4)) * 128, 128)
             out[:, pl.ds(lane, 128)] = jnp.transpose(block).astype(BF16)
+    for dz in DZ:
+        for which in (0, 1):
+            for t in (0, 1):
+                part_copy(dz, which, t, False)
 
 
 def per_device(tokens, context_row, lengths, qw, kw, vw, ow):

time: 83.1 us -> 82.9 us (level)
  no operation moved by 1% of the time
where the time goes in v5:
time: 82.9 us; the launch traced here: 82.8 us
  Pallas kernels  82.1 us (99%)
    pallas_call x1, Pallas kernels, per_device(): pl.pallas_call(body, out_shape=pltpu.VMEM((128, 1024), BF16), in_specs=[p...  82.1 us

profile of v5, /device:TPU:5, one launch (start us, length us, event | category | flops | bytes accessed | tf_op | source)
XLA Modules:
  0.0 82.8 jit_solution(1000401417916509656)
XLA Ops:
  0.0 82.1 %shard_map.73 = bf16[128,1024]{1,0:T(8,128)(2,1)S(1)} custom-call(bf16[128,1024]{1,0:T(8,128)(2,1)} %refs_0_.1, s32[64,128]{1,0:T(8,128)} %bitcast.4, s32[1,64]{1,0:T(1,128)} %bitcast.5, bf16[64,1024]{1,0:T(8,128)(2,1)} %refs_3_.1, bf16[64,128]{1,0:T(8,128)(2,1)} %refs_4_.1, bf16[64,128]{1,0:T(8,128)(2,1)} %refs_5_.1, bf16[64,1024]{1,0:T(8,128)(2,1)} %bitcast.3), custom_call_target="tpu_custom_call" | custom-call | tf_op jit(solution)/shard_map/pallas_call | solution.py:613
  82.1 0.7 copy.9

commit v6 on v5

--- a/solution.py
+++ b/solution.py
@@ -237,14 +237,6 @@
         local(5, ow.at[:, pl.ds(0, 384)], o1.at[0, 0]),
         local(6, ow.at[:, pl.ds(384, 640)], o2.at[0, 0]),
     ]
-    for copy in early + late:
-        copy.start()
-    for which in (0, 1):
-
-        @pl.when(core == which)
-        def _():
-            own_kv[which].start()
-
     peers = [across] + [at(0, 0, which, dx) for dx in (1, 2, 3) for which in (0, 1)]
     peers += [chip_at(by, other) for by in (1, 2, -1, -2)]
     barrier = pltpu.get_barrier_semaphore()
@@ -254,6 +246,14 @@
     @pl.loop(1, 32)
     def _(by):
         pl.semaphore_signal(barrier, inc=1, device_id=chip_at(by, core), device_id_type=MESH)
+
+    for copy in early + late:
+        copy.start()
+    for which in (0, 1):
+
+        @pl.when(core == which)
+        def _():
+            own_kv[which].start()
 
     for copy in early:
         copy.wait()

time: 82.9 us -> 82.8 us (level)
  no operation moved by 1% of the time
where the time goes in v6:
time: 82.8 us; the launch traced here: 82.7 us
  Pallas kernels  82 us (99%)
    pallas_call x1, Pallas kernels, per_device(): pl.pallas_call(body, out_shape=pltpu.VMEM((128, 1024), BF16), in_specs=[p...  82 us

profile of v6, /device:TPU:5, one launch (start us, length us, event | category | flops | bytes accessed | tf_op | source)
XLA Modules:
  0.0 82.7 jit_solution(12924115235559378575)
XLA Ops:
  0.0 82.0 %shard_map.73 = bf16[128,1024]{1,0:T(8,128)(2,1)S(1)} custom-call(bf16[128,1024]{1,0:T(8,128)(2,1)} %refs_0_.1, s32[64,128]{1,0:T(8,128)} %bitcast.4, s32[1,64]{1,0:T(1,128)} %bitcast.5, bf16[64,1024]{1,0:T(8,128)(2,1)} %refs_3_.1, bf16[64,128]{1,0:T(8,128)(2,1)} %refs_4_.1, bf16[64,128]{1,0:T(8,128)(2,1)} %refs_5_.1, bf16[64,1024]{1,0:T(8,128)(2,1)} %bitcast.3), custom_call_target="tpu_custom_call" | custom-call | tf_op jit(solution)/shard_map/pallas_call | solution.py:613
  82.0 0.7 copy.9
